TPU v7x, 32 devices: a whole 2x2x4 slice. The times are simulated.
32 devices in a mesh: dp: 8 (over z, x), ctx: 2 (over y), tensor: 2 (over core).
Axes of the slice: x: 2, y: 2, z: 4, core: 2. Of those that a mesh axis runs over, the one named last changes fastest.
Arguments:
- tokens: bfloat16 [8, 1024, 1024], P('dp', ('ctx', 'tensor')), may hold values from -6 to 6
- places: int32 [8, 1024], P('dp', 'ctx'), may hold values from 0 to 1023, as said below
- attn_gain: float32 [1024], P('dp'), may hold values from 0.25 to 1.75
- w_query: float32 [1024, 2048], P('dp', 'tensor'), may hold values from -0.1875 to 0.1875
- w_key: float32 [1024, 1024], P('dp', 'tensor'), may hold values from -0.1875 to 0.1875
- w_value: float32 [1024, 1024], P('dp', 'tensor'), may hold values from -0.1875 to 0.1875
- q_gain: float32 [128], P('dp'), may hold values from 1 to 2
- k_gain: float32 [128], P('dp'), may hold values from 1 to 2
- w_out: float32 [2048, 1024], P('tensor', 'dp'), may hold values from -1 to 1
- mlp_gain: float32 [1024], P('dp'), may hold values from 0.25 to 1.75
- w_gate: float32 [1024, 3072], P('dp', 'tensor'), may hold values from -0.1875 to 0.1875
- w_up: float32 [1024, 3072], P('dp', 'tensor'), may hold values from -0.1875 to 0.1875
- w_down: float32 [3072, 1024], P('tensor', 'dp'), may hold values from -0.109375 to 0.109375
- cotangent: bfloat16 [8, 1024, 1024], P('dp', ('ctx', 'tensor')), may hold values from -6 to 6
Outputs:
- out: float32 [8, 1024, 1024], P('dp', ('ctx', 'tensor'))
- grad_in: float32 [8, 1024, 1024], P('dp', ('ctx', 'tensor'))
- grad_attn_gain: float32 [1024], replicated
- grad_w_query: float32 [1024, 2048], P(('dp', 'ctx'), 'tensor')
- grad_w_key: float32 [1024, 1024], P(('dp', 'ctx'), 'tensor')
- grad_w_value: float32 [1024, 1024], P(('dp', 'ctx'), 'tensor')
- grad_q_gain: float32 [128], replicated
- grad_k_gain: float32 [128], replicated
- grad_w_out: float32 [2048, 1024], P('tensor', ('dp', 'ctx'))
- grad_mlp_gain: float32 [1024], replicated
- grad_w_gate: float32 [1024, 3072], P(('dp', 'ctx'), 'tensor')
- grad_w_up: float32 [1024, 3072], P(('dp', 'ctx'), 'tensor')
- grad_w_down: float32 [3072, 1024], P('tensor', ('dp', 'ctx'))
Inputs may be any that keep to these rules, and one draw needn't show every extreme that they name: Each row of places is a permutation of 0 to 1023: with n the number of ctx devices, the positions fall into 2 n runs of 1024 / (2 n) in a row, run k covering k * 1024 / (2 n) to (k + 1) * 1024 / (2 n) - 1; the stored tokens of ctx device c hold run c in their first half and run 2 n - 1 - c in their second half, in a drawn order within each run.
All inputs are finite; a program needn't handle non-finite values.
Results may differ from a plain program's by a relative error of at most 0.015.
The roundings to bfloat16 on the way count: a program that leaves them out, or rounds other values in their place, can miss the bound.
Values may be sent and summed in bfloat16 or wider, within the bound.
No kernel may reach another device: no remote copies, remote signals or barrier semaphores. Data moves between devices by JAX's collectives and lax.ppermute only.
A program may use at most 192 MiB of HBM per device.

v0:
```python
import jax
import jax.numpy as jnp
from jax import lax
from jax.sharding import PartitionSpec as P

HD = 128


EPSILON = 1e-06
ROPE_BASE = 1000000.0
NEGATIVE = -1e30


def gather_rows(source):
    return lax.all_gather(source, "tensor", axis=1, tiled=True)


def reduce_rows(partial_sum):
    return lax.psum_scatter(partial_sum, "tensor", scatter_dimension=1, tiled=True)


def norm_forward(source, gain):
    factor = lax.rsqrt(jnp.mean(source * source, axis=-1, keepdims=True) + EPSILON)
    unit = source * factor
    return (unit * gain, unit, factor)


def norm_backward(grad_normed, unit, factor, gain):
    grad_unit = grad_normed * gain
    grad_gain = jnp.sum((grad_normed * unit).reshape(-1, unit.shape[-1]), axis=0)
    grad_source = factor * (grad_unit - unit * jnp.mean(grad_unit * unit, axis=-1, keepdims=True))
    return (grad_source, grad_gain)


def rope_tables(positions):
    freq_index = jnp.arange(HD // 2, dtype=jnp.float32)
    inverse = ROPE_BASE ** (-2.0 * freq_index / HD)
    angles = positions.astype(jnp.float32)[..., None] * inverse
    cosine = jnp.concatenate([jnp.cos(angles), jnp.cos(angles)], axis=-1)
    sine_table = jnp.concatenate([jnp.sin(angles), jnp.sin(angles)], axis=-1)
    return (cosine[..., None, :], sine_table[..., None, :])


def rotate(source, cosine, sine_table):
    half_width = source.shape[-1] // 2
    turned = jnp.concatenate([-source[..., half_width:], source[..., :half_width]], axis=-1)
    return source * cosine + turned * sine_table


def rotate_back(grad_rotated, cosine, sine_table):
    half_width = grad_rotated.shape[-1] // 2
    sined = grad_rotated * sine_table
    turned = jnp.concatenate([sined[..., half_width:], -sined[..., :half_width]], axis=-1)
    return grad_rotated * cosine + turned


def to_blocks(heads_last, kv_heads):
    seqs, row_count, width = heads_last.shape
    group_size = width // (kv_heads * HD)
    shaped = heads_last.reshape(seqs, row_count, kv_heads, group_size, HD)
    return shaped.transpose(0, 2, 3, 1, 4).reshape(seqs * kv_heads, group_size, row_count, HD)


def from_blocks(blocked, seqs):
    count, group_size, row_count, width = blocked.shape
    kv_heads = count // seqs
    shaped = blocked.reshape(seqs, kv_heads, group_size, row_count, width)
    return shaped.transpose(0, 3, 1, 2, 4).reshape(seqs, row_count, kv_heads * group_size * width)


def masked_scores(queries, key_rows, query_places, key_places):
    scores = jnp.einsum(
        "hqd,kd->hqk", queries, key_rows, preferred_element_type=jnp.float32
    ) * HD ** (-0.5)
    visible = key_places[None, None, :] <= query_places[None, :, None]
    return jnp.where(visible, scores, NEGATIVE)


def recompute(queries, key_rows, lse_rows, query_places, key_places):
    return jnp.exp(masked_scores(queries, key_rows, query_places, key_places) - lse_rows[..., None])


def forward_block(pieces):
    queries, key_rows, value_rows, query_places, key_places = pieces
    scores = masked_scores(queries, key_rows, query_places, key_places)
    row_max = jnp.max(scores, axis=-1, keepdims=True)
    raised = jnp.exp(scores - row_max)
    row_total = jnp.sum(raised, axis=-1, keepdims=True)
    attn_probs = raised / row_total
    mixed = jnp.einsum(
        "hqk,kd->hqd",
        attn_probs.astype(jnp.bfloat16),
        value_rows,
        preferred_element_type=jnp.float32,
    )
    return (mixed, (row_max + jnp.log(row_total))[..., 0])


def full_block(pieces):
    queries, grad_mixed, lse_rows, query_places, key_rows, value_rows, key_places = pieces
    attn_probs = recompute(queries, key_rows, lse_rows, query_places, key_places)
    grad_probs = jnp.einsum(
        "hqd,kd->hqk", grad_mixed, value_rows, preferred_element_type=jnp.float32
    )
    row_delta = jnp.sum(attn_probs * grad_probs, axis=-1)
    grad_scores = (attn_probs * (grad_probs - row_delta[..., None])).astype(jnp.bfloat16)
    grad_queries = jnp.einsum(
        "hqk,kd->hqd", grad_scores, key_rows, preferred_element_type=jnp.float32
    ) * HD ** (-0.5)
    grad_keys = jnp.einsum(
        "hqk,hqd->kd", grad_scores, queries, preferred_element_type=jnp.float32
    ) * HD ** (-0.5)
    grad_values = jnp.einsum(
        "hqk,hqd->kd",
        attn_probs.astype(jnp.bfloat16),
        grad_mixed,
        preferred_element_type=jnp.float32,
    )
    return (grad_queries, grad_keys, grad_values)


def body(
    tokens,
    places,
    attn_gain,
    w_query,
    w_key,
    w_value,
    q_gain,
    k_gain,
    w_out,
    mlp_gain,
    w_gate,
    w_up,
    w_down,
    cotangent,
):
    seqs, local_rows, width = tokens.shape
    attn_set = (
        lax.all_gather(attn_gain.astype(jnp.bfloat16), "dp", axis=0, tiled=True),
        lax.all_gather(w_query.astype(jnp.bfloat16), "dp", axis=0, tiled=True),
        lax.all_gather(w_key.astype(jnp.bfloat16), "dp", axis=0, tiled=True),
        lax.all_gather(w_value.astype(jnp.bfloat16), "dp", axis=0, tiled=True),
        lax.all_gather(q_gain.astype(jnp.bfloat16), "dp", axis=0, tiled=True),
        lax.all_gather(k_gain.astype(jnp.bfloat16), "dp", axis=0, tiled=True),
        lax.all_gather(w_out.astype(jnp.bfloat16), "dp", axis=1, tiled=True),
    )
    gain_one, query_weight, key_weight, value_weight, query_gain, key_gain, out_weight = attn_set
    mlp_set = (
        lax.all_gather(mlp_gain.astype(jnp.bfloat16), "dp", axis=0, tiled=True),
        lax.all_gather(w_gate.astype(jnp.bfloat16), "dp", axis=0, tiled=True),
        lax.all_gather(w_up.astype(jnp.bfloat16), "dp", axis=0, tiled=True),
        lax.all_gather(w_down.astype(jnp.bfloat16), "dp", axis=1, tiled=True),
    )
    gain_two, gate_weight, up_weight, down_weight = mlp_set
    gain_one = gain_one.astype(jnp.float32)
    gain_two = gain_two.astype(jnp.float32)
    query_gain = query_gain.astype(jnp.float32)
    key_gain = key_gain.astype(jnp.float32)
    source = tokens.astype(jnp.float32)
    normed_one, unit_one, factor_one = norm_forward(source, gain_one)
    rows_one = gather_rows(normed_one.astype(jnp.bfloat16))
    group_rows = rows_one.shape[1]
    flat_one = rows_one.reshape(seqs * group_rows, width)
    query_raw = jnp.dot(flat_one, query_weight, preferred_element_type=jnp.float32).reshape(
        seqs, group_rows, -1, HD
    )
    key_raw = jnp.dot(flat_one, key_weight, preferred_element_type=jnp.float32).reshape(
        seqs, group_rows, -1, HD
    )
    value_rows = (
        jnp.dot(flat_one, value_weight, preferred_element_type=jnp.float32)
        .astype(jnp.bfloat16)
        .reshape(seqs, group_rows, -1)
    )
    kv_heads = key_raw.shape[2]
    cosine, sine_table = rope_tables(places)
    query_normed, query_unit, query_factor = norm_forward(query_raw, query_gain)
    queries = (
        rotate(query_normed, cosine, sine_table).astype(jnp.bfloat16).reshape(seqs, group_rows, -1)
    )
    key_normed, key_unit, key_factor = norm_forward(key_raw, key_gain)
    key_rows = (
        rotate(key_normed, cosine, sine_table).astype(jnp.bfloat16).reshape(seqs, group_rows, -1)
    )
    key_all, value_all, places_all = (
        lax.all_gather(key_rows, "ctx", axis=1, tiled=True),
        lax.all_gather(value_rows, "ctx", axis=1, tiled=True),
        lax.all_gather(places, "ctx", axis=1, tiled=True),
    )
    query_blocks = to_blocks(queries, kv_heads)
    key_blocks = to_blocks(key_all, kv_heads)[:, 0]
    value_blocks = to_blocks(value_all, kv_heads)[:, 0]
    query_places = jnp.repeat(places, kv_heads, axis=0)
    key_places = jnp.repeat(places_all, kv_heads, axis=0)
    mixed_blocks, lse_blocks = lax.map(
        forward_block, (query_blocks, key_blocks, value_blocks, query_places, key_places)
    )
    mixed = from_blocks(mixed_blocks, seqs).astype(jnp.bfloat16).reshape(seqs * group_rows, -1)
    attn_part = jnp.dot(mixed, out_weight, preferred_element_type=jnp.float32).reshape(
        seqs, group_rows, width
    )
    middle = source + reduce_rows(attn_part)
    normed_two, unit_two, factor_two = norm_forward(middle, gain_two)
    rows_two = gather_rows(normed_two.astype(jnp.bfloat16)).reshape(seqs * group_rows, width)
    gate_act = jnp.dot(rows_two, gate_weight, preferred_element_type=jnp.float32)
    up_act = jnp.dot(rows_two, up_weight, preferred_element_type=jnp.float32)
    sigmoid_gate = jax.nn.sigmoid(gate_act)
    silu_gate = gate_act * sigmoid_gate
    hidden = (silu_gate * up_act).astype(jnp.bfloat16)
    mlp_part = jnp.dot(hidden, down_weight, preferred_element_type=jnp.float32).reshape(
        seqs, group_rows, width
    )
    layer_out = middle + reduce_rows(mlp_part)
    grad_rows = gather_rows(cotangent).reshape(seqs * group_rows, width)
    down_grad = jnp.einsum("tf,td->fd", hidden, grad_rows, preferred_element_type=jnp.float32)
    grad_hidden = jnp.einsum(
        "td,fd->tf", grad_rows, down_weight, preferred_element_type=jnp.float32
    )
    grad_gate = (
        grad_hidden * up_act * sigmoid_gate * (1.0 + gate_act * (1.0 - sigmoid_gate))
    ).astype(jnp.bfloat16)
    grad_up = (grad_hidden * silu_gate).astype(jnp.bfloat16)
    gate_grad = jnp.einsum("td,tf->df", rows_two, grad_gate, preferred_element_type=jnp.float32)
    up_grad = jnp.einsum("td,tf->df", rows_two, grad_up, preferred_element_type=jnp.float32)
    grad_normed_two = jnp.einsum(
        "tf,df->td", grad_gate, gate_weight, preferred_element_type=jnp.float32
    ) + jnp.einsum("tf,df->td", grad_up, up_weight, preferred_element_type=jnp.float32)
    grad_normed_two = reduce_rows(grad_normed_two.reshape(seqs, group_rows, width))
    grad_source_two, grad_gain_two = norm_backward(grad_normed_two, unit_two, factor_two, gain_two)
    grad_middle = cotangent.astype(jnp.float32) + grad_source_two
    grad_branch = gather_rows(grad_middle.astype(jnp.bfloat16)).reshape(seqs * group_rows, width)
    out_grad = jnp.einsum("tc,td->cd", mixed, grad_branch, preferred_element_type=jnp.float32)
    grad_mixed = (
        jnp.einsum("td,cd->tc", grad_branch, out_weight, preferred_element_type=jnp.float32)
        .astype(jnp.bfloat16)
        .reshape(seqs, group_rows, -1)
    )
    grad_blocks = to_blocks(grad_mixed, kv_heads)
    grad_query_blocks, grad_key_blocks, grad_value_blocks = lax.map(
        full_block,
        (query_blocks, grad_blocks, lse_blocks, query_places, key_blocks, value_blocks, key_places),
    )
    key_terms = jnp.concatenate(
        [
            from_blocks(grad_key_blocks[:, None], seqs),
            from_blocks(grad_value_blocks[:, None], seqs),
        ],
        axis=-1,
    )
    key_sums = lax.psum_scatter(
        key_terms.astype(jnp.bfloat16), "ctx", scatter_dimension=1, tiled=True
    ).astype(jnp.float32)
    half_width = key_sums.shape[-1] // 2
    grad_keys = key_sums[..., :half_width]
    grad_values = key_sums[..., half_width:]
    grad_query_rot = from_blocks(grad_query_blocks, seqs).reshape(seqs, group_rows, -1, HD)
    grad_query_raw, grad_q_part = norm_backward(
        rotate_back(grad_query_rot, cosine, sine_table), query_unit, query_factor, query_gain
    )
    grad_query_raw = grad_query_raw.astype(jnp.bfloat16).reshape(seqs * group_rows, -1)
    grad_key_rot = grad_keys.reshape(seqs, group_rows, kv_heads, HD)
    grad_key_raw, grad_k_part = norm_backward(
        rotate_back(grad_key_rot, cosine, sine_table), key_unit, key_factor, key_gain
    )
    grad_key_raw = grad_key_raw.astype(jnp.bfloat16).reshape(seqs * group_rows, -1)
    grad_value_raw = grad_values.astype(jnp.bfloat16).reshape(seqs * group_rows, -1)
    query_grad = jnp.einsum(
        "td,tc->dc", flat_one, grad_query_raw, preferred_element_type=jnp.float32
    )
    key_grad = jnp.einsum("td,tc->dc", flat_one, grad_key_raw, preferred_element_type=jnp.float32)
    value_grad = jnp.einsum(
        "td,tc->dc", flat_one, grad_value_raw, preferred_element_type=jnp.float32
    )
    grad_normed_one = jnp.einsum(
        "tc,dc->td", grad_query_raw, query_weight, preferred_element_type=jnp.float32
    )
    grad_normed_one = grad_normed_one + jnp.einsum(
        "tc,dc->td", grad_key_raw, key_weight, preferred_element_type=jnp.float32
    )
    grad_normed_one = grad_normed_one + jnp.einsum(
        "tc,dc->td", grad_value_raw, value_weight, preferred_element_type=jnp.float32
    )
    grad_normed_one = reduce_rows(grad_normed_one.reshape(seqs, group_rows, width))
    grad_source_one, grad_gain_one = norm_backward(grad_normed_one, unit_one, factor_one, gain_one)
    grad_tokens = grad_middle + grad_source_one
    weight_grads = (
        lax.psum_scatter(query_grad, ("dp", "ctx"), scatter_dimension=0, tiled=True),
        lax.psum_scatter(key_grad, ("dp", "ctx"), scatter_dimension=0, tiled=True),
        lax.psum_scatter(value_grad, ("dp", "ctx"), scatter_dimension=0, tiled=True),
        lax.psum_scatter(out_grad, ("dp", "ctx"), scatter_dimension=1, tiled=True),
        lax.psum_scatter(gate_grad, ("dp", "ctx"), scatter_dimension=0, tiled=True),
        lax.psum_scatter(up_grad, ("dp", "ctx"), scatter_dimension=0, tiled=True),
        lax.psum_scatter(down_grad, ("dp", "ctx"), scatter_dimension=1, tiled=True),
    )
    gain_grads = lax.psum(
        (grad_gain_one, grad_q_part, grad_k_part, grad_gain_two), ("dp", "ctx", "tensor")
    )
    return (
        layer_out,
        grad_tokens,
        gain_grads[0],
        weight_grads[0],
        weight_grads[1],
        weight_grads[2],
        gain_grads[1],
        gain_grads[2],
        weight_grads[3],
        gain_grads[3],
        weight_grads[4],
        weight_grads[5],
        weight_grads[6],
    )


def solution(mesh):
    in_specs = (
        P("dp", ("ctx", "tensor"), None),
        P("dp", "ctx"),
        P("dp"),
        P("dp", "tensor"),
        P("dp", "tensor"),
        P("dp", "tensor"),
        P("dp"),
        P("dp"),
        P("tensor", "dp"),
        P("dp"),
        P("dp", "tensor"),
        P("dp", "tensor"),
        P("tensor", "dp"),
        P("dp", ("ctx", "tensor"), None),
    )
    out_specs = (
        P("dp", ("ctx", "tensor"), None),
        P("dp", ("ctx", "tensor"), None),
        P(),
        P(("dp", "ctx"), "tensor"),
        P(("dp", "ctx"), "tensor"),
        P(("dp", "ctx"), "tensor"),
        P(),
        P(),
        P("tensor", ("dp", "ctx")),
        P(),
        P(("dp", "ctx"), "tensor"),
        P(("dp", "ctx"), "tensor"),
        P("tensor", ("dp", "ctx")),
    )
    return jax.shard_map(body, mesh=mesh, in_specs=in_specs, out_specs=out_specs, check_vma=False)
```

profile of v0, /device:TPU:0, one launch (start us, length us, event | category | flops | bytes accessed | tf_op | source)
XLA Modules:
  0.0 1500.2 jit_solution(15128395107612899023)
XLA Ops:
  8.0 22.1 %all-gather.2 = bf16[8,1,128]{2,1,0:T(2,128)(2,1)S(1)} all-gather(bf16[1,1,128]{2,1,0:T(2,128)(2,1)S(1)} %convert_bitcast_fusion.3), channel_id=1, replica_groups=mesh['dp'=8,'ctx'=2,'tensor'=2] {'dp'}, dimensions={0}, use_global_device_ids=true | all-gather | bytes 2304 | tf_op jit(solution)/shard_map/all_gather | solution.py:140
  36.8 17.1 %all-reduce.3 = (bf16[128]{0:T(256)(128)(2,1)S(1)}, bf16[128]{0:T(256)(128)(2,1)S(1)}) all-reduce(bf16[128]{0:T(256)(128)(2,1)S(1)} %dynamic-update-slice, bf16[128]{0:T(256)(128)(2,1)S(1)} %dynamic-update-slice.1), channel_id=1, replica_groups=mesh['dp'=8,'ctx'=2,'tensor'=2] {'dp'}, use_global_device_ids=true, to_apply=%add | all-reduce | flops 256 | bytes 1024
  56.9 27.0 %all-gather.22.cloned.1.call-done = bf16[1024,512]{1,0:T(8,128)(2,1)} async-done(((bf16[128,512]{1,0:T(8,128)(2,1)}), bf16[1024,512]{1,0:T(8,128)(2,1)}) %all-gather.22.cloned.1.call-update) | async-done | bytes 1048592 | tf_op jit(solution)/shard_map/all_gather | solution.py:142
  91.7 33.9 %all-gather.24.cloned.1.call-done = bf16[1024,512]{1,0:T(8,128)(2,1)} async-done(((bf16[128,512]{1,0:T(8,128)(2,1)}), bf16[1024,512]{1,0:T(8,128)(2,1)}) %all-gather.24.cloned.1.call-update) | async-done | bytes 1048592 | tf_op jit(solution)/shard_map/all_gather | solution.py:143
  130.0 4.6 all_gather.56
  134.7 13.0 all-gather.40.cloned.1.call-done
  149.9 21.0 %all-gather.42.cloned.1.call-done = bf16[1024,512]{1,0:T(8,128)(2,1)} async-done(((bf16[512,512]{1,0:T(8,128)(2,1)}), bf16[1024,512]{1,0:T(8,128)(2,1)}) %all-gather.42.cloned.1.call-update) | async-done | bytes 1048592 | tf_op jit(solution)/shard_map/all_gather | solution.py:188
  173.4 49.4 %all-gather.20.cloned.1.call-done = bf16[1024,1024]{1,0:T(8,128)(2,1)} async-done(((bf16[128,1024]{1,0:T(8,128)(2,1)}), bf16[1024,1024]{1,0:T(8,128)(2,1)}) %all-gather.20.cloned.1.call-update) | async-done | bytes 2097168 | tf_op jit(solution)/shard_map/all_gather | solution.py:141
  236.5 3.3 copy.136
  239.8 3.6 fusion.106
  243.4 29.2 %while.26 = (s32[]{:T(128)}, bf16[4,2,512,128]{2,3,1,0:T(8,128)(2,1)}, f32[4,2,512]{2,1,0:T(2,128)S(1)}, s32[4,1024]{1,0:T(4,128)S(1)}, s32[4,512]{1,0:T(4,128)S...) while((s32[]{:T(128)}, ...), condition=%wide.region_6.7_spmd, body=%wide.region_3.6_spmd.sunk | while | flops 549977088 | bytes 24432800 | solution.py:196
  275.1 4.5 convolution_bitcast_fusion.1
  281.6 17.6 %all-gather.3 = bf16[8,1,128]{2,1,0:T(2,128)(2,1)S(1)} all-gather(bf16[1,1,128]{2,1,0:T(2,128)(2,1)S(1)} %convert_bitcast_fusion.2), channel_id=1, replica_groups=mesh['dp'=8,'ctx'=2,'tensor'=2] {'dp'}, dimensions={0}, use_global_device_ids=true | all-gather | bytes 2304 | tf_op jit(solution)/shard_map/all_gather | solution.py:150
  304.6 47.6 %all-gather.32.cloned.1.call-done = bf16[1024,1536]{1,0:T(8,128)(2,1)} async-done(((bf16[128,1536]{1,0:T(8,128)(2,1)}), bf16[1024,1536]{1,0:T(8,128)(2,1)}) %all-gather.32.cloned.1.call-update) | async-done | bytes 3145744 | tf_op jit(solution)/shard_map/all_gather | solution.py:152
  352.2 9.7 all-gather.28.cloned.1.call-done
  361.9 5.7 fusion.91
  367.6 58.9 %all-gather.30.cloned.1.call-done = bf16[1024,1536]{1,0:T(8,128)(2,1)} async-done(((bf16[128,1536]{1,0:T(8,128)(2,1)}), bf16[1024,1536]{1,0:T(8,128)(2,1)}) %all-gather.30.cloned.1.call-update) | async-done | bytes 3145744 | tf_op jit(solution)/shard_map/all_gather | solution.py:151
  426.6 5.4 fusion.93
  432.0 3.7 all-gather.36.cloned.1.call-done
  435.7 67.1 %all-gather.34.cloned.1.call-done = bf16[1536,1024]{1,0:T(8,128)(2,1)} async-done(((bf16[1536,128]{1,0:T(8,128)(2,1)}), bf16[1536,1024]{1,0:T(8,128)(2,1)}) %all-gather.34.cloned.1.call-update) | async-done | bytes 3145744 | tf_op jit(solution)/shard_map/all_gather | solution.py:153
  502.8 8.3 multiply_convert_fusion.1
  514.1 3.2 add_bitcast_fusion.1
  517.4 7.9 reduce-scatter.17.cloned.1.call-done
  528.5 10.1 all-gather.38.cloned.1.call-done
  538.6 4.2 convolution_convert_fusion
  547.8 51.7 %while.27 = (s32[]{:T(128)}, f32[4,2,512,128]{3,2,1,0:T(8,128)S(1)}, bf16[4,1024,128]{2,1,0:T(8,128)(2,1)}, bf16[4,1024,128]{2,1,0:T(8,128)(2,1)}, s32[4,1024]{1...) while((s32[]{:T(128)}, ...), condition=%wide.region_14.15_spmd, body=%wide.region_12.14_spmd.sunk | while | flops 1358691328 | bytes 49597652 | solution.py:240
  604.0 3.1 pad_maximum_fusion.1
  617.5 3.0 copy.147
  620.5 4.1 reshape_reshape.10
  636.3 3.9 reduce-scatter.19.cloned.1.call-done
  644.3 4.0 multiply_reduce_fusion.5
  657.8 5.5 convolution_bitcast_fusion.2
  664.8 5.9 fusion.89
  670.7 6.0 fusion.87
  678.0 5.9 fusion.83
  685.1 3.1 fusion.97
  688.3 3.1 fusion.95
  691.5 4.8 fusion.80
  696.6 4.6 fusion.99
  714.3 40.4 %all-reduce.2 = (f32[1024]{0:T(1024)}, f32[128]{0:T(128)}, f32[128]{0:T(128)}, f32[1024]{0:T(1024)}) all-reduce(f32[1024]{0:T(1024)S(1)} %get-tuple-element.124, f32[128]{0:T(128)S(1)} %get-tuple-element.120, f32[128]{0:T(128)S(1)} %fusion.79, ...), channel_id=1, replica_groups=mesh['dp'=8,'ctx'=2,'tensor'=2] {'dp','ctx','tensor'}, use_global_device_ids=true, to_apply=%region_21.22 | all-reduce | flops 2304 | bytes 18432 | tf_op jit(solution)/shard_map/psum | solution.py:296
  754.7 3.4 fusion.69
  758.1 76.1 %reduce-scatter.31.cloned.1.call-done = f32[64,1536]{1,0:T(8,128)} async-done(((f32[1024,1536]{1,0:T(8,128)}), f32[64,1536]{1,0:T(8,128)}) %reduce-scatter.31.cloned.1.call-update) | async-done | bytes 393232 | tf_op jit(solution)/shard_map/reduce_scatter | solution.py:292
  834.1 151.4 %reduce-scatter.33.cloned.1.call-done = f32[64,1536]{1,0:T(8,128)} async-done(((f32[1024,1536]{1,0:T(8,128)}), f32[64,1536]{1,0:T(8,128)}) %reduce-scatter.33.cloned.1.call-update) | async-done | bytes 393232 | tf_op jit(solution)/shard_map/reduce_scatter | solution.py:293
  985.6 152.0 %reduce-scatter.35.cloned.1.call-done = f32[1536,64]{0,1:T(8,128)} async-done(((f32[1536,1024]{0,1:T(8,128)}), f32[1536,64]{0,1:T(8,128)}) %reduce-scatter.35.cloned.1.call-update) | async-done | bytes 393232 | tf_op jit(solution)/shard_map/reduce_scatter | solution.py:294
  1137.5 83.1 %reduce-scatter.25.cloned.1.call-done = f32[64,512]{1,0:T(8,128)} async-done(((f32[1024,512]{1,0:T(8,128)}), f32[64,512]{1,0:T(8,128)}) %reduce-scatter.25.cloned.1.call-update) | async-done | bytes 131088 | tf_op jit(solution)/shard_map/reduce_scatter | solution.py:289
  1220.7 80.8 %reduce-scatter.27.cloned.1.call-done = f32[64,512]{1,0:T(8,128)} async-done(((f32[1024,512]{1,0:T(8,128)}), f32[64,512]{1,0:T(8,128)}) %reduce-scatter.27.cloned.1.call-update) | async-done | bytes 131088 | tf_op jit(solution)/shard_map/reduce_scatter | solution.py:290
  1301.4 95.1 %reduce-scatter.29.cloned.1.call-done = f32[1024,64]{0,1:T(8,128)} async-done(((f32[1024,1024]{0,1:T(8,128)}), f32[1024,64]{0,1:T(8,128)}) %reduce-scatter.29.cloned.1.call-update) | async-done | bytes 262160 | tf_op jit(solution)/shard_map/reduce_scatter | solution.py:291
  1396.5 97.0 %reduce-scatter.23.cloned.1.call-done = f32[64,1024]{1,0:T(8,128)} async-done(((f32[1024,1024]{1,0:T(8,128)}), f32[64,1024]{1,0:T(8,128)}) %reduce-scatter.23.cloned.1.call-update) | async-done | bytes 262160 | tf_op jit(solution)/shard_map/reduce_scatter | solution.py:288
  (410 shorter events, 198.5 us)
Async XLA Ops:
  7.2 27.9 %copy-start.72 = (u32[32]{0:T(128)S(1)}, u32[32]{0:T(128)}, u32[]{:S(2)}) copy-start(u32[32]{0:T(128)} %constant.89) | copy-start | bytes 388
  7.2 26.3 %copy-start.50 = (f32[128,512]{1,0:T(8,128)S(1)}, f32[128,512]{1,0:T(8,128)}, u32[]{:S(2)}) copy-start(f32[128,512]{1,0:T(8,128)} %param.22) | copy-start | bytes 786436
  7.2 27.0 %copy-start.51 = (f32[128,512]{1,0:T(8,128)S(1)}, f32[128,512]{1,0:T(8,128)}, u32[]{:S(2)}) copy-start(f32[128,512]{1,0:T(8,128)} %param.23) | copy-start | bytes 786436
  7.2 27.8 %copy-start.69 = (f32[16]{0:T(128)S(1)}, f32[16]{0:T(128)}, u32[]{:S(2)}) copy-start(f32[16]{0:T(128)} %param.24) | copy-start | bytes 196
  7.2 27.8 %copy-start.70 = (f32[16]{0:T(128)S(1)}, f32[16]{0:T(128)}, u32[]{:S(2)}) copy-start(f32[16]{0:T(128)} %param.25) | copy-start | bytes 196
  7.2 46.7 %copy-start.56 = (s32[1,512]{1,0:T(1,128)S(1)}, s32[1,512]{1,0:T(1,128)}, u32[]{:S(2)}) copy-start(s32[1,512]{1,0:T(1,128)} %param.19) | copy-start | bytes 6148
  7.2 49.7 %all-gather.18.cloned.1.call-start = ((), (), s32[]{:S(2)}) async-start(), calls=%async_computation.12 | async-start | bytes 1572864 | tf_op jit(solution)/shard_map/all_gather | solution.py:15
  30.1 23.8 %copy-start.54 = (f32[8,1,128]{2,1,0:T(1,128)}, f32[8,1,128]{2,1,0:T(1,128)S(1)}, u32[]{:S(2)}) copy-start(f32[8,1,128]{2,1,0:T(1,128)S(1)} %convert_element_type.187) | copy-start | bytes 12292
  31.4 22.6 %copy-start.59 = (f32[256]{0:T(256)}, f32[256]{0:T(256)S(1)}, u32[]{:S(2)}) copy-start(f32[256]{0:T(256)S(1)} %add_rsqrt_fusion.3) | copy-start | bytes 3076
  33.4 50.5 %all-gather.22.cloned.1.call-start = ((), (), s32[]{:S(2)}) async-start(), calls=%async_computation.14 | async-start | bytes 1179648 | tf_op jit(solution)/shard_map/all_gather | solution.py:142
  34.2 91.4 %all-gather.24.cloned.1.call-start = ((), (), s32[]{:S(2)}) async-start(), calls=%async_computation.15 | async-start | bytes 1179648 | tf_op jit(solution)/shard_map/all_gather | solution.py:143
  34.9 112.7 %all-gather.40.cloned.1.call-start = ((), (), s32[]{:S(2)}) async-start(), calls=%async_computation.35 | async-start | bytes 1572864 | tf_op jit(solution)/shard_map/all_gather | solution.py:187
  53.9 33.0 %copy-start.61 = (f32[128]{0:T(128)}, f32[128]{0:T(128)S(1)}, u32[]{:S(2)}) copy-start(f32[128]{0:T(128)S(1)} %convert_element_type.163) | copy-start | bytes 1540
  56.9 32.4 %copy-start.57 = (f32[512]{0:T(512)}, f32[512]{0:T(512)S(1)}, u32[]{:S(2)}) copy-start(f32[512]{0:T(512)S(1)} %broadcast_bitcast_fusion.1) | copy-start | bytes 6148
  89.3 36.2 %copy-start.12 = (bf16[1,512,1024]{2,1,0:T(8,128)(2,1)S(1)}, bf16[1,512,1024]{2,1,0:T(8,128)(2,1)}, u32[]{:S(2)}) copy-start(bf16[1,512,1024]{2,1,0:T(8,128)(2,1)} %all-gather.18.cloned.1.call-done) | copy-start | bytes 3145732
  91.7 36.7 %copy-start.48 = (f32[128,1024]{1,0:T(8,128)S(1)}, f32[128,1024]{1,0:T(8,128)}, u32[]{:S(2)}) copy-start(f32[128,1024]{1,0:T(8,128)} %param.21) | copy-start | bytes 1572868
  91.7 37.5 %copy-start.49 = (f32[1024,128]{1,0:T(8,128)S(1)}, f32[1024,128]{1,0:T(8,128)}, u32[]{:S(2)}) copy-start(f32[1024,128]{1,0:T(8,128)} %param.26) | copy-start | bytes 1572868
  91.7 79.3 %all-gather.42.cloned.1.call-start = ((), (), s32[]{:S(2)}) async-start(), calls=%async_computation.36 | async-start | bytes 1572864 | tf_op jit(solution)/shard_map/all_gather | solution.py:188
  128.3 94.5 %all-gather.20.cloned.1.call-start = ((), (), s32[]{:S(2)}) async-start(), calls=%async_computation.13 | async-start | bytes 2359296 | tf_op jit(solution)/shard_map/all_gather | solution.py:141
  129.2 145.9 %all-gather.26.cloned.1.call-start = ((), (), s32[]{:S(2)}) async-start(), calls=%async_computation.16 | async-start | bytes 2359296 | tf_op jit(solution)/shard_map/all_gather | solution.py:146
  130.0 169.2 %reduce-scatter.13.cloned.1.call-start = ((), (), s32[]{:S(2)}) async-start(), calls=%async_computation.17 | async-start | bytes 3145728 | tf_op jit(solution)/shard_map/reduce_scatter | solution.py:19
  149.9 72.9 %copy-start.13 = (bf16[1,512,1024]{2,1,0:T(8,128)(2,1)S(1)}, bf16[1,512,1024]{2,1,0:T(8,128)(2,1)}, u32[]{:S(2)}) copy-start(bf16[1,512,1024]{2,1,0:T(8,128)(2,1)} %all-gather.18.cloned.1.call-done) | copy-start | bytes 3145732
  279.6 19.6 %copy-start.10 = (bf16[1,256,1024]{2,1,0:T(8,128)(2,1)S(1)}, bf16[1,256,1024]{2,1,0:T(8,128)(2,1)}, u32[]{:S(2)}) copy-start(bf16[1,256,1024]{2,1,0:T(8,128)(2,1)} %param.18) | copy-start | bytes 1572868
  279.6 72.6 %all-gather.32.cloned.1.call-start = ((), (), s32[]{:S(2)}) async-start(), calls=%async_computation.20 | async-start | bytes 3538944 | tf_op jit(solution)/shard_map/all_gather | solution.py:152
  281.5 80.4 %all-gather.28.cloned.1.call-start = ((), (), s32[]{:S(2)}) async-start(), calls=%async_computation.18 | async-start | bytes 1572864 | tf_op jit(solution)/shard_map/all_gather | solution.py:15
  301.7 124.8 %all-gather.30.cloned.1.call-start = ((), (), s32[]{:S(2)}) async-start(), calls=%async_computation.19 | async-start | bytes 3538944 | tf_op jit(solution)/shard_map/all_gather | solution.py:151
  302.6 133.1 %all-gather.36.cloned.1.call-start = ((), (), s32[]{:S(2)}) async-start(), calls=%async_computation.23 | async-start | bytes 1572864 | tf_op jit(solution)/shard_map/all_gather | solution.py:15
  303.2 199.6 %all-gather.34.cloned.1.call-start = ((), (), s32[]{:S(2)}) async-start(), calls=%async_computation.21 | async-start | bytes 3538944 | tf_op jit(solution)/shard_map/all_gather | solution.py:153
  304.1 221.3 %reduce-scatter.17.cloned.1.call-start = ((), (), s32[]{:S(2)}) async-start(), calls=%async_computation.24 | async-start | bytes 3145728 | tf_op jit(solution)/shard_map/reduce_scatter | solution.py:19
  361.9 64.6 %copy-start.66 = (bf16[1,512,1024]{2,1,0:T(8,128)(2,1)S(1)}, bf16[1,512,1024]{2,1,0:T(8,128)(2,1)}, u32[]{:S(2)}) copy-start(bf16[1,512,1024]{2,1,0:T(8,128)(2,1)} %all-gather.28.cloned.1.call-done) | copy-start | bytes 3145732
  502.8 8.3 copy-start.64
  517.4 9.7 copy-start.29
  517.4 21.2 %all-gather.38.cloned.1.call-start = ((), (), s32[]{:S(2)}) async-start(), calls=%async_computation.25 | async-start | bytes 1572864 | tf_op jit(solution)/shard_map/all_gather | solution.py:15
  528.2 112.0 %reduce-scatter.19.cloned.1.call-start = ((), (), s32[]{:S(2)}) async-start(), calls=%async_computation.26 | async-start | bytes 3145728 | tf_op jit(solution)/shard_map/reduce_scatter | solution.py:251
  607.1 105.4 %reduce-scatter.21.cloned.1.call-start = ((), (), s32[]{:S(2)}) async-start(), calls=%async_computation.27 | async-start | bytes 3145728 | tf_op jit(solution)/shard_map/reduce_scatter | solution.py:19
  620.5 4.1 copy-start.7
  643.9 4.5 copy-start.21
  643.9 4.5 copy-start.23
  657.7 96.9 %reduce-scatter.15.cloned.1.call-start = ((), (), s32[]{:S(2)}) async-start(), calls=%async_computation.22 | async-start | bytes 3145728 | tf_op jit(solution)/shard_map/reduce_scatter | solution.py:19
  663.3 170.8 %reduce-scatter.31.cloned.1.call-start = ((), (), s32[]{:S(2)}) async-start(), calls=%async_computation.32 | async-start | bytes 6684672 | tf_op jit(solution)/shard_map/reduce_scatter | solution.py:292
  670.7 314.9 %reduce-scatter.33.cloned.1.call-start = ((), (), s32[]{:S(2)}) async-start(), calls=%async_computation.33 | async-start | bytes 6684672 | tf_op jit(solution)/shard_map/reduce_scatter | solution.py:293
  676.7 460.8 %reduce-scatter.35.cloned.1.call-start = ((), (), s32[]{:S(2)}) async-start(), calls=%async_computation.34 | async-start | bytes 6684672 | tf_op jit(solution)/shard_map/reduce_scatter | solution.py:294
  683.9 536.8 %reduce-scatter.25.cloned.1.call-start = ((), (), s32[]{:S(2)}) async-start(), calls=%async_computation.29 | async-start | bytes 2228224 | tf_op jit(solution)/shard_map/reduce_scatter | solution.py:289
  688.2 613.2 %reduce-scatter.27.cloned.1.call-start = ((), (), s32[]{:S(2)}) async-start(), calls=%async_computation.30 | async-start | bytes 2228224 | tf_op jit(solution)/shard_map/reduce_scatter | solution.py:290
  691.4 705.1 %reduce-scatter.29.cloned.1.call-start = ((), (), s32[]{:S(2)}) async-start(), calls=%async_computation.31 | async-start | bytes 4456448 | tf_op jit(solution)/shard_map/reduce_scatter | solution.py:291
  696.3 797.1 %reduce-scatter.23.cloned.1.call-start = ((), (), s32[]{:S(2)}) async-start(), calls=%async_computation.28 | async-start | bytes 4456448 | tf_op jit(solution)/shard_map/reduce_scatter | solution.py:288
  709.8 44.9 %copy-start.30 = (bf16[1,256,1024]{2,1,0:T(8,128)(2,1)S(1)}, bf16[1,256,1024]{2,1,0:T(8,128)(2,1)}, u32[]{:S(2)}) copy-start(bf16[1,256,1024]{2,1,0:T(8,128)(2,1)} %param.31) | copy-start | bytes 1572868
  712.4 42.2 %copy-start.20 = (f32[1,256,1024]{2,1,0:T(8,128)S(1)}, f32[1,256,1024]{2,1,0:T(8,128)}, u32[]{:S(2)}) copy-start(f32[1,256,1024]{2,1,0:T(8,128)} %reduce-scatter.17.cloned.1.call-done) | copy-start | bytes 3145732
  (67 other events, 123.8 us)
Sparse Core Ops, SparseCore 0:
  33.5 6.3 all-gather.17
  42.6 41.3 all-gather.21
  86.6 38.8 all-gather.23
  127.6 20.0 all-gather.39
  149.6 21.2 all-gather.41
  173.5 49.2 all-gather.19
  225.5 49.5 all-gather.25
  279.7 7.7 reduce-scatter.12
  290.5 61.5 all-gather.31
  354.2 7.6 all-gather.27
  364.9 61.5 all-gather.29
  428.0 7.6 all-gather.35
  438.5 64.2 all-gather.33
  517.5 7.7 reduce-scatter.16
  528.4 10.1 all-gather.37
  607.2 32.9 reduce-scatter.18
  657.9 9.5 reduce-scatter.20
  669.6 10.7 reduce-scatter.14
  687.0 147.0 reduce-scatter.30
  840.6 144.8 reduce-scatter.32
  992.2 145.2 reduce-scatter.34
  1140.5 80.1 reduce-scatter.24
  1223.6 77.7 reduce-scatter.26
  1304.3 92.1 reduce-scatter.28
  1399.5 93.9 reduce-scatter.22
where the time goes:
time: 1510 us; the launch traced here: 1500 us
  waiting for transfers between devices  1090 us (72%)
  matrix products  145 us (10%)
  blocking collectives  102 us (7%)
  local copies, waits for them, and re-layouts  72.9 us (5%)
  other arithmetic  70.1 us (5%)
  between operations  15.9 us (1%)
    reduce_scatter x1, waiting for transfers between devices, body(): lax.psum_scatter(down_grad, ('dp', 'ctx'), scatter_dimension=1, tiled=True)  152 us
    reduce_scatter x1, waiting for transfers between devices, body(): lax.psum_scatter(up_grad, ('dp', 'ctx'), scatter_dimension=0, tiled=True)  151 us
    reduce_scatter x1, waiting for transfers between devices, body(): lax.psum_scatter(query_grad, ('dp', 'ctx'), scatter_dimension=0, tiled=True)  97 us
    reduce_scatter x1, waiting for transfers between devices, body(): lax.psum_scatter(out_grad, ('dp', 'ctx'), scatter_dimension=1, tiled=True)  95.1 us
    reduce_scatter x1, waiting for transfers between devices, body(): lax.psum_scatter(key_grad, ('dp', 'ctx'), scatter_dimension=0, tiled=True)  83.1 us
    reduce_scatter x1, waiting for transfers between devices, body(): lax.psum_scatter(value_grad, ('dp', 'ctx'), scatter_dimension=0, tiled=True)  80.8 us
    reduce_scatter x1, waiting for transfers between devices, body(): lax.psum_scatter(gate_grad, ('dp', 'ctx'), scatter_dimension=0, tiled=True)  76.1 us
    all_gather x1, waiting for transfers between devices, body(): lax.all_gather(w_down.astype(jnp.bfloat16), 'dp', axis=1, tiled=True)  67.1 us
  transfers between devices with their start and end apart: 25, of which 21 were waited for; matrix products, arithmetic and copies ran while one was open for 11% of the time, Pallas kernels for 0%

commit v1 on v0

--- a/solution.py
+++ b/solution.py
@@ -1,6 +1,10 @@
+import functools
+
 import jax
 import jax.numpy as jnp
 from jax import lax
+from jax.experimental import pallas as pl
+from jax.experimental.pallas import tpu as pltpu
 from jax.sharding import PartitionSpec as P
 
 HD = 128
@@ -119,7 +123,7 @@
     return (grad_queries, grad_keys, grad_values)
 
 
-def body(
+def split_body(
     tokens,
     places,
     attn_gain,
@@ -313,6 +317,425 @@
     )
 
 
+NT = (((1,), (1,)), ((), ()))
+TN = (((0,), (0,)), ((), ()))
+NN = (((1,), (0,)), ((), ()))
+SCALE = HD ** (-0.5)
+
+
+def dot(left, right, dims=NN):
+    return lax.dot_general(left, right, dims, preferred_element_type=jnp.float32)
+
+
+def sort_runs(block_of, run, *pairs):
+    for index in range(4):
+        source = pl.multiple_of(block_of[index] * run, run)
+        for target, origin in pairs:
+            target[pl.ds(index * run, run), :] = origin[pl.ds(source, run), :]
+
+
+def raw_scores(keys, query, visible, run):
+    scores = dot(keys, query, NT) * SCALE
+    count = scores.shape[0]
+    last = jnp.where(visible, scores[count - run :], NEGATIVE)
+    if count == run:
+        return last
+    return jnp.concatenate([scores[: count - run], last], axis=0)
+
+
+def forward_kernel(
+    block_of, q_ref, k_ref, v_ref, column_ref, row_ref, mixed_ref, lse_ref, keys, values, columns
+):
+    run = q_ref.shape[0] // 4
+    sort_runs(block_of, run, (keys, k_ref), (values, v_ref), (columns, column_ref))
+    for index in range(4):
+        count = run * (index + 1)
+        rows = pl.ds(pl.multiple_of(block_of[index] * run, run), run)
+        visible = columns[pl.ds(count - run, run), :] <= row_ref[:, rows]
+        for head in range(q_ref.shape[1] // HD):
+            lanes = pl.ds(head * HD, HD)
+            scores = raw_scores(keys[:count], q_ref[rows, lanes], visible, run)
+            row_max = jnp.max(scores, axis=0, keepdims=True)
+            raised = jnp.exp(scores - row_max)
+            row_total = jnp.sum(raised, axis=0, keepdims=True)
+            probs = (raised * (1.0 / row_total)).astype(jnp.bfloat16)
+            mixed_ref[rows, lanes] = dot(probs, values[:count], TN).astype(jnp.bfloat16)
+            lse_ref[pl.ds(head, 1), rows] = row_max + jnp.log(row_total)
+
+
+def backward_kernel(
+    block_of,
+    q_ref,
+    k_ref,
+    v_ref,
+    g_ref,
+    lse_ref,
+    column_ref,
+    row_ref,
+    dq_ref,
+    dk_ref,
+    dv_ref,
+    keys,
+    values,
+    columns,
+    key_sum,
+    value_sum,
+):
+    run = q_ref.shape[0] // 4
+    sort_runs(block_of, run, (keys, k_ref), (values, v_ref), (columns, column_ref))
+    key_sum[...] = jnp.zeros_like(key_sum)
+    value_sum[...] = jnp.zeros_like(value_sum)
+    for index in range(4):
+        count = run * (index + 1)
+        rows = pl.ds(pl.multiple_of(block_of[index] * run, run), run)
+        visible = columns[pl.ds(count - run, run), :] <= row_ref[:, rows]
+        for head in range(q_ref.shape[1] // HD):
+            lanes = pl.ds(head * HD, HD)
+            query = q_ref[rows, lanes]
+            grad = g_ref[rows, lanes]
+            scores = raw_scores(keys[:count], query, visible, run)
+            probs = jnp.exp(scores - lse_ref[pl.ds(head, 1), rows])
+            grad_probs = dot(values[:count], grad, NT)
+            delta = jnp.sum(probs * grad_probs, axis=0, keepdims=True)
+            grad_scores = (probs * (grad_probs - delta)).astype(jnp.bfloat16)
+            value_sum[:count, :] += dot(probs.astype(jnp.bfloat16), grad)
+            key_sum[:count, :] += dot(grad_scores, query)
+            dq_ref[rows, lanes] = dot(grad_scores, keys[:count], TN) * SCALE
+    for index in range(4):
+        rows = pl.ds(pl.multiple_of(block_of[index] * run, run), run)
+        dk_ref[rows, :] = key_sum[pl.ds(index * run, run), :] * SCALE
+        dv_ref[rows, :] = value_sum[pl.ds(index * run, run), :]
+
+
+def head_spec(rows, width):
+    return pl.BlockSpec((rows, width), lambda group, order: (0, group))
+
+
+def attend(block_of, queries, keys, values, place_column, place_row):
+    rows, width = keys.shape
+    groups = width // HD
+    pair = queries.shape[1] // groups
+    fixed_column = pl.BlockSpec((rows, 1), lambda group, order: (0, 0))
+    fixed_row = pl.BlockSpec((1, rows), lambda group, order: (0, 0))
+    lse_spec = pl.BlockSpec((None, pair // HD, rows), lambda group, order: (group, 0, 0))
+    return pl.pallas_call(
+        forward_kernel,
+        grid_spec=pltpu.PrefetchScalarGridSpec(
+            num_scalar_prefetch=1,
+            grid=(groups,),
+            in_specs=[
+                head_spec(rows, pair),
+                head_spec(rows, HD),
+                head_spec(rows, HD),
+                fixed_column,
+                fixed_row,
+            ],
+            out_specs=[head_spec(rows, pair), lse_spec],
+            scratch_shapes=[
+                pltpu.VMEM((rows, HD), jnp.bfloat16),
+                pltpu.VMEM((rows, HD), jnp.bfloat16),
+                pltpu.VMEM((rows, 1), jnp.int32),
+            ],
+        ),
+        out_shape=[
+            jax.ShapeDtypeStruct(queries.shape, jnp.bfloat16),
+            jax.ShapeDtypeStruct((groups, pair // HD, rows), jnp.float32),
+        ],
+        compiler_params=pltpu.CompilerParams(vmem_limit_bytes=40 * 1024 * 1024),
+        cost_estimate=pl.CostEstimate(
+            flops=3 * rows * rows * queries.shape[1],
+            bytes_accessed=8 * rows * queries.shape[1],
+            transcendentals=rows * rows * queries.shape[1] // HD,
+        ),
+    )(block_of, queries, keys, values, place_column, place_row)
+
+
+def attend_back(block_of, queries, keys, values, grad_mixed, lse_rows, place_column, place_row):
+    rows, width = keys.shape
+    groups = width // HD
+    pair = queries.shape[1] // groups
+    fixed_column = pl.BlockSpec((rows, 1), lambda group, order: (0, 0))
+    fixed_row = pl.BlockSpec((1, rows), lambda group, order: (0, 0))
+    lse_spec = pl.BlockSpec((None, pair // HD, rows), lambda group, order: (group, 0, 0))
+    return pl.pallas_call(
+        backward_kernel,
+        grid_spec=pltpu.PrefetchScalarGridSpec(
+            num_scalar_prefetch=1,
+            grid=(groups,),
+            in_specs=[
+                head_spec(rows, pair),
+                head_spec(rows, HD),
+                head_spec(rows, HD),
+                head_spec(rows, pair),
+                lse_spec,
+                fixed_column,
+                fixed_row,
+            ],
+            out_specs=[head_spec(rows, pair), head_spec(rows, HD), head_spec(rows, HD)],
+            scratch_shapes=[
+                pltpu.VMEM((rows, HD), jnp.bfloat16),
+                pltpu.VMEM((rows, HD), jnp.bfloat16),
+                pltpu.VMEM((rows, 1), jnp.int32),
+                pltpu.VMEM((rows, HD), jnp.float32),
+                pltpu.VMEM((rows, HD), jnp.float32),
+            ],
+        ),
+        out_shape=[
+            jax.ShapeDtypeStruct(queries.shape, jnp.float32),
+            jax.ShapeDtypeStruct(keys.shape, jnp.float32),
+            jax.ShapeDtypeStruct(keys.shape, jnp.float32),
+        ],
+        compiler_params=pltpu.CompilerParams(vmem_limit_bytes=40 * 1024 * 1024),
+        cost_estimate=pl.CostEstimate(
+            flops=7 * rows * rows * queries.shape[1],
+            bytes_accessed=16 * rows * queries.shape[1],
+            transcendentals=rows * rows * queries.shape[1] // HD,
+        ),
+    )(block_of, queries, keys, values, grad_mixed, lse_rows, place_column, place_row)
+
+
+def swap(source, axis, size, bit=1):
+    return lax.ppermute(source, axis, [(i, i ^ bit) for i in range(size)])
+
+
+def group_body(
+    dp_size,
+    tokens,
+    places,
+    attn_gain,
+    w_query,
+    w_key,
+    w_value,
+    q_gain,
+    k_gain,
+    w_out,
+    mlp_gain,
+    w_gate,
+    w_up,
+    w_down,
+    cotangent,
+):
+    bf16, f32 = jnp.bfloat16, jnp.float32
+    run, width = tokens.shape[1:]
+    side = lax.axis_index("ctx")
+    core = lax.axis_index("tensor")
+    member = lax.axis_index("dp")
+
+    def over_core(source):
+        return swap(source, "tensor", 2)
+
+    def over_ctx(source):
+        return swap(source, "ctx", 2)
+
+    def spread(own):
+        half = jnp.concatenate([own, over_ctx(own)], axis=0)
+        return jnp.concatenate([half, over_core(half)], axis=0)
+
+    def core_sum(parts):
+        half = parts.shape[0] // 2
+        return parts[:half] + over_core(parts[half:].astype(bf16)).astype(f32)
+
+    def own_sum(parts):
+        summed = core_sum(parts)
+        return summed[:run] + over_ctx(summed[run:].astype(bf16)).astype(f32)
+
+    def half_sum(parts):
+        summed = core_sum(parts)
+        other = over_ctx(summed.astype(bf16)).astype(f32)
+        return summed + jnp.concatenate([other[run:], other[:run]], axis=0)
+
+    def mine(source, axis):
+        size = source.shape[axis] // 2
+        return lax.dynamic_slice_in_dim(source, side * size, size, axis).astype(bf16)
+
+    def gather_small(source):
+        bit = 1
+        while bit < dp_size:
+            other = swap(source, "dp", dp_size, bit)
+            first = (member // bit) % 2 == 0
+            source = jnp.where(
+                first,
+                jnp.concatenate([source, other], axis=0),
+                jnp.concatenate([other, source], axis=0),
+            )
+            bit *= 2
+        return source
+
+    def sum_small(source):
+        source = source + over_core(source)
+        source = source + over_ctx(source)
+        bit = 1
+        while bit < dp_size:
+            source = source + swap(source, "dp", dp_size, bit)
+            bit *= 2
+        return source
+
+    gain_block = attn_gain.shape[0]
+    head_block = q_gain.shape[0]
+    gains = gather_small(
+        jnp.concatenate([attn_gain, mlp_gain, q_gain, k_gain]).astype(bf16)[None]
+    ).astype(f32)
+    gain_one = gains[:, :gain_block].reshape(-1)
+    gain_two = gains[:, gain_block : 2 * gain_block].reshape(-1)
+    query_gain = gains[:, 2 * gain_block : 2 * gain_block + head_block].reshape(-1)
+    key_gain = gains[:, 2 * gain_block + head_block :].reshape(-1)
+
+    attn_shard = jnp.concatenate(
+        [mine(w_query, 1), mine(w_key, 1), mine(w_value, 1), mine(w_out, 0).T], axis=1
+    )
+    mlp_shard = jnp.concatenate([mine(w_gate, 1), mine(w_up, 1), mine(w_down, 0).T], axis=1)
+    attn_weight = lax.all_gather(attn_shard, "dp", axis=0, tiled=True)
+    mlp_weight = lax.all_gather(mlp_shard, "dp", axis=0, tiled=True)
+    q_width = w_query.shape[1] // 2
+    k_width = w_key.shape[1] // 2
+    kv_end = q_width + 2 * k_width
+    hidden_width = w_gate.shape[1] // 2
+    qkv_weight = attn_weight[:, :kv_end]
+    out_weight = attn_weight[:, kv_end:]
+    gate_up_weight = mlp_weight[:, : 2 * hidden_width]
+    down_weight = mlp_weight[:, 2 * hidden_width :]
+
+    rows_all = spread(tokens[0])
+    source = rows_all.astype(f32)
+    grad_rows = spread(cotangent[0])
+    other_places = over_ctx(places)[0].reshape(2, run)
+    own_places = places[0].reshape(2, run)
+    place_blocks = jnp.stack([own_places, other_places], axis=1)
+    place_blocks = jnp.where(core == 0, place_blocks, place_blocks[::-1]).reshape(-1)
+    place_column = place_blocks[:, None]
+    place_row = place_blocks[None, :]
+    home_side = jnp.array([0, 1, 1, 0], jnp.int32)
+    home_core = jnp.array([0, 0, 1, 1], jnp.int32)
+    block_of = (home_core ^ core) * 2 + (home_side ^ side)
+
+    normed_one, unit_one, factor_one = norm_forward(source, gain_one)
+    normed_one = normed_one.astype(bf16)
+    projected = dot(normed_one, qkv_weight)
+    row_count = projected.shape[0]
+    query_raw = projected[:, :q_width].reshape(row_count, -1, HD)
+    key_raw = projected[:, q_width : q_width + k_width].reshape(row_count, -1, HD)
+    value_rows = projected[:, q_width + k_width :].astype(bf16)
+    cosine, sine_table = rope_tables(place_blocks)
+    query_normed, query_unit, query_factor = norm_forward(query_raw, query_gain)
+    queries = rotate(query_normed, cosine, sine_table).astype(bf16).reshape(row_count, -1)
+    key_normed, key_unit, key_factor = norm_forward(key_raw, key_gain)
+    key_rows = rotate(key_normed, cosine, sine_table).astype(bf16).reshape(row_count, -1)
+    mixed, lse_rows = attend(block_of, queries, key_rows, value_rows, place_column, place_row)
+
+    middle = source[: 2 * run] + half_sum(dot(mixed, out_weight, NT))
+    normed_two, unit_two, factor_two = norm_forward(middle, gain_two)
+    normed_two = normed_two.astype(bf16)
+    rows_two = jnp.concatenate([normed_two, over_core(normed_two)], axis=0)
+    gate_up = dot(rows_two, gate_up_weight)
+    gate_act = gate_up[:, :hidden_width]
+    up_act = gate_up[:, hidden_width:]
+    sigmoid_gate = jax.nn.sigmoid(gate_act)
+    silu_gate = gate_act * sigmoid_gate
+    hidden = (silu_gate * up_act).astype(bf16)
+    grad_hidden = dot(grad_rows, down_weight)
+    grad_gate = (
+        grad_hidden * up_act * sigmoid_gate * (1.0 + gate_act * (1.0 - sigmoid_gate))
+    ).astype(bf16)
+    grad_up = (grad_hidden * silu_gate).astype(bf16)
+    grad_gate_up = jnp.concatenate([grad_gate, grad_up], axis=1)
+    layer_out = middle[:run] + own_sum(dot(hidden, down_weight, NT))
+
+    grad_normed_two = half_sum(dot(grad_gate_up, gate_up_weight, NT))
+    mlp_grad = jnp.concatenate(
+        [
+            dot(rows_two, grad_gate_up, TN).astype(bf16),
+            dot(grad_rows, hidden, TN).astype(bf16),
+        ],
+        axis=1,
+    )
+    grad_source_two, _ = norm_backward(grad_normed_two, unit_two, factor_two, gain_two)
+    grad_gain_two = jnp.sum(grad_normed_two[:run] * unit_two[:run], axis=0)
+    grad_middle = grad_rows[: 2 * run].astype(f32) + grad_source_two
+    branch_half = grad_middle.astype(bf16)
+    grad_branch = jnp.concatenate([branch_half, over_core(branch_half)], axis=0)
+    grad_mixed = dot(grad_branch, out_weight).astype(bf16)
+    grad_query_rot, grad_key_rot, grad_values = attend_back(
+        block_of, queries, key_rows, value_rows, grad_mixed, lse_rows, place_column, place_row
+    )
+    grad_query_raw, grad_q_part = norm_backward(
+        rotate_back(grad_query_rot.reshape(row_count, -1, HD), cosine, sine_table),
+        query_unit,
+        query_factor,
+        query_gain,
+    )
+    grad_key_raw, grad_k_part = norm_backward(
+        rotate_back(grad_key_rot.reshape(row_count, -1, HD), cosine, sine_table),
+        key_unit,
+        key_factor,
+        key_gain,
+    )
+    grad_qkv = jnp.concatenate(
+        [
+            grad_query_raw.astype(bf16).reshape(row_count, -1),
+            grad_key_raw.astype(bf16).reshape(row_count, -1),
+            grad_values.astype(bf16),
+        ],
+        axis=1,
+    )
+    attn_grad = jnp.concatenate(
+        [dot(normed_one, grad_qkv, TN).astype(bf16), dot(grad_branch, mixed, TN).astype(bf16)],
+        axis=1,
+    )
+    grad_normed_one = own_sum(dot(grad_qkv, qkv_weight, NT))
+    grad_source_one, grad_gain_one = norm_backward(
+        grad_normed_one, unit_one[:run], factor_one[:run], gain_one
+    )
+    grad_tokens = grad_middle[:run] + grad_source_one
+
+    def owned(grad):
+        block = lax.psum_scatter(grad, "dp", scatter_dimension=0, tiled=True)
+        size = block.shape[0] // 2
+        kept = lax.dynamic_slice_in_dim(block, side * size, size, 0)
+        sent = lax.dynamic_slice_in_dim(block, (1 - side) * size, size, 0)
+        return kept.astype(f32), over_ctx(sent).astype(f32)
+
+    def joined(kept, other):
+        return jnp.where(
+            side == 0,
+            jnp.concatenate([kept, other], axis=1),
+            jnp.concatenate([other, kept], axis=1),
+        )
+
+    mlp_kept, mlp_other = owned(mlp_grad)
+    attn_kept, attn_other = owned(attn_grad)
+
+    def part(pair, start, stop):
+        return joined(pair[0][:, start:stop], pair[1][:, start:stop])
+
+    attn_pair = (attn_kept, attn_other)
+    mlp_pair = (mlp_kept, mlp_other)
+    gain_grads = sum_small(
+        jnp.concatenate([grad_gain_one, grad_gain_two, grad_q_part, grad_k_part])
+    )
+    return (
+        layer_out[None],
+        grad_tokens[None],
+        gain_grads[:width],
+        part(attn_pair, 0, q_width),
+        part(attn_pair, q_width, q_width + k_width),
+        part(attn_pair, q_width + k_width, kv_end),
+        gain_grads[2 * width : 2 * width + HD],
+        gain_grads[2 * width + HD :],
+        part(attn_pair, kv_end, attn_kept.shape[1]).T,
+        gain_grads[width : 2 * width],
+        part(mlp_pair, 0, hidden_width),
+        part(mlp_pair, hidden_width, 2 * hidden_width),
+        part(mlp_pair, 2 * hidden_width, mlp_kept.shape[1]).T,
+    )
+
+
+def plan(mesh):
+    sizes = dict(mesh.shape)
+    if sizes["ctx"] == 2 and sizes["tensor"] == 2 and sizes["dp"] & (sizes["dp"] - 1) == 0:
+        return functools.partial(group_body, sizes["dp"])
+    return split_body
+
+
 def solution(mesh):
     in_specs = (
         P("dp", ("ctx", "tensor"), None),
@@ -345,4 +768,4 @@
         P(("dp", "ctx"), "tensor"),
         P("tensor", ("dp", "ctx")),
     )
-    return jax.shard_map(body, mesh=mesh, in_specs=in_specs, out_specs=out_specs, check_vma=False)
+    return jax.shard_map(plan(mesh), mesh=mesh, in_specs=in_specs, out_specs=out_specs, check_vma=False)

time: 1510 us -> 398 us (0.26)
  waiting for transfers between devices: 1090 us -> 152 us
  matrix products: 145 us -> 42.5 us
  blocking collectives: 102 us -> 0 us
  starting transfers between devices: 1.91 us -> 24.5 us
  Pallas kernels: 0 us -> 19.2 us
    reduce_scatter x12 -> x1, waiting for transfers between devices: 747 us -> 0.01 us  [owned(): block = lax.psum_scatter(grad, 'dp', scatter_dimension=0, tiled=True)]
    all_gather x13 -> x2, waiting for transfers between devices: 344 us -> 43.6 us  [the longest x1 43.6 us: group_body(): attn_weight = lax.all_gather(attn_shard, 'dp', axis=0, tiled=True)]
    dot_general x49 -> x12, matrix products: 145 us -> 42.5 us  [dot(): lax.dot_general(left, right, dims, preferred_element_type=jnp.float32)]
    ppermute x0 -> x25, waiting for transfers between devices: none -> 98 us  [swap(): return lax.ppermute(source, axis, [(i, i ^ bit) for i in range(size)])]
    all_gather x3 -> x0, blocking collectives: 44.3 us -> none  [the longest x1 22.1 us: body(): lax.all_gather(attn_gain.astype(jnp.bfloat16), 'dp', axis=0, tiled=True)]
    psum x1 -> x0, blocking collectives: 40.4 us -> none  [body(): lax.psum((grad_gain_one, grad_q_part, grad_k_part, grad_gain_two), ('dp',...]
    ppermute x0 -> x25, starting transfers between devices: none -> 24.3 us  [swap(): return lax.ppermute(source, axis, [(i, i ^ bit) for i in range(size)])]
    pallas_call x0 -> x2, Pallas kernels: none -> 19.2 us  [the longest x1 11.9 us: attend_back(): pl.pallas_call(backward_kernel, grid_spec=pltpu.PrefetchScalarGridSpec(nu...]
  transfers between devices with their start and end apart: 25 -> 29, of which waited for: 21 -> 16; matrix products, arithmetic and copies ran while one was open for 11% -> 38% of each run, Pallas kernels for 0% -> 5%
where the time goes in v1:
time: 398 us; the launch traced here: 391 us
  waiting for transfers between devices  152 us (38%)
  other arithmetic  75.3 us (19%)
  local copies, waits for them, and re-layouts  61.4 us (15%)
  matrix products  42.5 us (11%)
  starting transfers between devices  24.5 us (6%)
  Pallas kernels  19.2 us (5%)
  between operations  15.7 us (4%)
    ppermute x25, waiting for transfers between devices, swap(): return lax.ppermute(source, axis, [(i, i ^ bit) for i in range(size)])  98 us
    all_gather x1, waiting for transfers between devices, group_body(): attn_weight = lax.all_gather(attn_shard, 'dp', axis=0, tiled=True)  43.6 us
    dot_general x12, matrix products, dot(): lax.dot_general(left, right, dims, preferred_element_type=jnp.float32)  42.5 us
    unnamed x223, local copies, waits for them, and re-layouts  25.7 us
    ppermute x25, starting transfers between devices, swap(): return lax.ppermute(source, axis, [(i, i ^ bit) for i in range(size)])  24.3 us
    pallas_call x1, Pallas kernels, attend_back(): pl.pallas_call(backward_kernel, grid_spec=pltpu.PrefetchScalarGridSpec(nu...  11.9 us
    unnamed x5, waiting for transfers between devices  10.4 us
    reduce_sum x3, other arithmetic, norm_backward(): jnp.mean(grad_unit * unit, axis=-1, keepdims=True)  9.35 us
  transfers between devices with their start and end apart: 29, of which 16 were waited for; matrix products, arithmetic and copies ran while one was open for 38% of the time, Pallas kernels for 5%

profile of v1, /device:TPU:0, one launch (start us, length us, event | category | flops | bytes accessed | tf_op | source)
XLA Modules:
  0.0 390.6 jit_solution(13732831309215216464)
XLA Ops:
  11.8 2.9 collective-permute-start.2
  21.0 2.0 collective-permute-done.3
  23.0 2.7 collective-permute-start.4
  33.8 43.6 %all-gather.3.cloned.1.call-done = bf16[1024,1536]{0,1:T(8,128)(2,1)} async-done(((bf16[128,1536]{0,1:T(8,128)(2,1)}), bf16[1024,1536]{0,1:T(8,128)(2,1)}) %all-gather.3.cloned.1.call-update) | async-done | bytes 3145744 | tf_op jit(solution)/shard_map/all_gather | solution.py:587
  77.5 4.0 %fusion.14 = f32[1024,1024]{1,0:T(8,128)S(1)} fusion(bf16[1024,1536]{0,1:T(8,128)(2,1)} %all-gather.3.cloned.1.call-done, f32[1024]{0:T(1024)S(1)} %get-tuple-element.117, f32[1024]{0:T(1024)S(1)} %add_rsqrt_fusion.2, bf16[512,1024]{1,0:T(8,128)(2,1)S(1)} %collective-permute-done.1, bf16[256,1024]{1,0:T(8,128)(2,1)S(1)} %collective-permute-done, ...), kind=kOutput, calls=%fused_computation.59 | convolution fusion | flops 2156920832 | bytes 8396800 | tf_op jit(solution)/shard_map/dot_general | solution.py:327
  87.7 2.1 reshape.244
  91.9 2.4 multiply_multiply_fusion.1
  96.8 2.4 multiply_multiply_fusion
  109.0 7.3 %shard_map.255 = (bf16[1024,512]{1,0:T(8,128)(2,1)S(1)}, f32[2,2,1024]{2,1,0:T(2,128)S(1)}) custom-call(s32[4]{0:T(128)S(1)} %xor_add_fusion.block_of, bf16[1024,512]{1,0:T(8,128)(2,1)S(1)} %fusion.9.q_ref, bf16[1024,256]{1,0:T(8,128)(2,1)S(1)} %fusion.26.k_ref, bf16[1024,256]{1,0:T(8,128)(2,1)S(1)} %slice.400.v_ref, s32[1024,1]{1,0:T(8,128)S(1)} %reshape.255.column_ref, ...), custom_call_target="tpu_custom_call" | custom-call | flops 1610612736 | bytes 4194304 | tf_op jit(solution)/shard_map/pallas_call | solution.py:421
  116.4 2.9 fusion.34
  119.6 2.6 collective-permute-done.6
  124.7 23.2 %collective-permute-done.7 = bf16[512,1024]{1,0:T(8,128)(2,1)S(1)} collective-permute-done((bf16[512,1024]{1,0:T(8,128)(2,1)S(1)}, bf16[512,1024]{1,0:T(8,128)(2,1)S(1)}, u32[]{:S(2)}, u32[]{:S(2)}) %collective-permute-start.7) | collective-permute-done | bytes 1048608 | tf_op jit(solution)/shard_map/ppermute | solution.py:498
  151.8 12.8 %collective-permute-done.11 = bf16[256,1024]{1,0:T(8,128)(2,1)S(1)} collective-permute-done((bf16[256,1024]{1,0:T(8,128)(2,1)S(1)}, bf16[256,1024]{1,0:T(8,128)(2,1)S(1)}, u32[]{:S(2)}, u32[]{:S(2)}) %collective-permute-start.11) | collective-permute-done | bytes 524320 | tf_op jit(solution)/shard_map/ppermute | solution.py:498
  165.7 6.1 %fusion.3 = f32[1024,1536]{1,0:T(8,128)S(1)} fusion(bf16[1024,2304]{0,1:T(8,128)(2,1)} %all-gather.5.cloned.1.call-done, bf16[512,1024]{1,0:T(8,128)(2,1)} %collective-permute-done.8, bf16[512,1024]{1,0:T(8,128)(2,1)} %get-tuple-element.72), kind=kOutput, calls=%fused_computation.13 | convolution fusion | flops 3225419776 | bytes 11534336 | tf_op jit(solution)/shard_map/dot_general | solution.py:327
  171.9 4.2 %multiply_convert_fusion.2 = (bf16[1024,768]{1,0:T(8,128)(2,1)S(1)}, bf16[1024,768]{1,0:T(8,128)(2,1)S(1)}, bf16[1024,768]{1,0:T(8,128)(2,1)S(1)}) fusion(f32[1024,1536]{1,0:T(8,128)S(1)} %fusion.3, bf16[1024,2304]{0,1:T(8,128)(2,1)S(1)} %copy-done.100, bf16[512,1024]{1,0:T(8,128)(2,1)} %collective-permute-done.12, ...), kind=kOutput, calls=%fused_computation.7 | convolution fusion | flops 1628700672 | bytes 14680064 | tf_op jit(solution)/shard_map/dot_general | solution.py:327
  176.1 3.4 fusion.1
  179.5 1.9 copy-done.70
  183.2 3.3 convolution_convert_fusion.2
  186.5 5.6 %convolution_convert_fusion = bf16[1024,1536]{1,0:T(8,128)(2,1)S(1)} fusion(bf16[1024,768]{1,0:T(8,128)(2,1)S(1)} %get-tuple-element.79, bf16[1024,768]{1,0:T(8,128)(2,1)S(1)} %get-tuple-element.78, bf16[512,1024]{1,0:T(8,128)(2,1)} %collective-permute-done.8, bf16[512,1024]{1,0:T(8,128)(2,1)} %get-tuple-element.72), kind=kOutput, calls=%fused_computation.3 | convolution fusion | flops 3233284096 | bytes 8388608 | tf_op jit(solution)/shard_map/dot_general | solution.py:327
  192.1 2.5 pad_maximum_fusion
  194.7 1.9 fusion.21
  198.2 23.9 %collective-permute-done.14 = bf16[512,1024]{1,0:T(8,128)(2,1)S(1)} collective-permute-done((bf16[512,1024]{1,0:T(8,128)(2,1)S(1)}, bf16[512,1024]{1,0:T(8,128)(2,1)S(1)}, u32[]{:S(2)}, u32[]{:S(2)}) %collective-permute-start.14) | collective-permute-done | bytes 1048608 | tf_op jit(solution)/shard_map/ppermute | solution.py:498
  225.5 2.6 collective-permute-done.15
  228.2 2.9 convolution_convert_fusion.4.g_ref
  231.1 11.9 %shard_map.256 = (f32[1024,512]{1,0:T(8,128)S(1)}, f32[1024,256]{1,0:T(8,128)S(1)}, f32[1024,256]{1,0:T(8,128)S(1)}) custom-call(s32[4]{0:T(128)S(1)} %xor_add_fusion.block_of, bf16[1024,512]{1,0:T(8,128)(2,1)S(1)} %copy-done.3, bf16[1024,256]{1,0:T(8,128)(2,1)S(1)} %copy-done.5, bf16[1024,256]{1,0:T(8,128)(2,1)S(1)} %copy-done.9, ...), custom_call_target="tpu_custom_call" | custom-call | flops 3758096384 | bytes 8388608 | tf_op jit(solution)/shard_map/pallas_call | solution.py:460
  247.1 1.9 broadcast_multiply_fusion.3
  251.0 4.2 %multiply_reduce_fusion.7 = (f32[1024,2]{1,0:T(8,128)S(1)}, f32[1024,2,128]{2,1,0:T(2,128)S(1)}) fusion(f32[1024,2,128]{2,1,0:T(2,128)S(1)} %copy-done.52, f32[1024,2,128]{2,1,0:T(2,128)S(1)} %copy-done.34, f32[128]{0:T(128)S(1)} %mul.429, f32[1024,128]{1,0:T(8,128)S(1)} %copy-done.42, f32[1024,2]{1,0:T(8,128)S(1)} %copy-done.46, ...), kind=kLoop, calls=%fused_computation.104 | loop fusion | flops 1832960 | bytes 4735488 | tf_op jit(solution)/shard_map/reduce_sum | solution.py:35
  257.5 4.6 %multiply_reduce_fusion.1 = (f32[1024,4]{1,0:T(8,128)S(1)}, f32[1024,4,128]{2,1,0:T(4,128)S(1)}) fusion(f32[1024,4,128]{2,1,0:T(4,128)S(1)} %copy-done.24, f32[1024,4,128]{2,1,0:T(4,128)S(1)} %copy-done.16, f32[128]{0:T(128)S(1)} %mul.408, f32[1024,128]{1,0:T(8,128)S(1)} %copy-done.42, f32[1024,4]{1,0:T(8,128)S(1)} %copy-done.40, ...), kind=kLoop, calls=%fused_computation.49 | loop fusion | flops 3665920 | bytes 8946176 | tf_op jit(solution)/shard_map/reduce_sum | solution.py:35
  269.7 2.6 convolution_convert_fusion.1
  272.3 2.0 pad_maximum_fusion.2
  274.4 4.9 %copy.87 = bf16[1024,1536]{1,0:T(8,128)(2,1)} copy(bf16[1024,1536]{0,1:T(8,128)(2,1)} %pad_maximum_fusion.2) | data formatting | bytes 6291456
  279.3 3.8 fusion.18
  286.2 2.3 fusion.12
  288.6 2.1 copy-done.74
  292.5 2.4 broadcast_multiply_fusion
  295.0 2.3 reshape.252
  298.5 2.7 reshape.250
  302.5 2.3 slice_add_fusion.2
  311.3 2.3 slice_add_fusion
  314.3 3.0 fusion.32
  318.1 2.5 fusion.11
  320.6 12.0 %collective-permute-done.17 = bf16[256,1024]{1,0:T(8,128)(2,1)S(1)} collective-permute-done((bf16[256,1024]{1,0:T(8,128)(2,1)S(1)}, bf16[256,1024]{1,0:T(8,128)(2,1)S(1)}, u32[]{:S(2)}, u32[]{:S(2)}) %collective-permute-start.17) | collective-permute-done | bytes 524320 | tf_op jit(solution)/shard_map/ppermute | solution.py:498
  337.2 2.1 collective-permute-done.19
  340.9 2.6 fusion.30
  343.6 3.7 collective-permute-done.21
  348.3 3.1 fusion.28
  355.8 10.3 %reduce-scatter.7.cloned.1.call-done = bf16[128,1536]{1,0:T(8,128)(2,1)} async-done(((bf16[1024,1536]{1,0:T(8,128)(2,1)}), bf16[128,1536]{1,0:T(8,128)(2,1)}) %reduce-scatter.7.cloned.1.call-update) | async-done | bytes 393232
  369.2 8.7 %collective-permute-done.23 = bf16[64,1536]{0,1:T(8,128)(2,1)S(1)} collective-permute-done((bf16[64,1536]{0,1:T(8,128)(2,1)S(1)}, bf16[64,1536]{0,1:T(8,128)(2,1)S(1)}, u32[]{:S(2)}, u32[]{:S(2)}) %collective-permute-start.23) | collective-permute-done | bytes 196640 | tf_op jit(solution)/shard_map/ppermute | solution.py:498
  (378 shorter events, 105.1 us)
Async XLA Ops:
  7.2 11.0 %copy-start = (f32[1536,128]{1,0:T(8,128)S(1)}, f32[1536,128]{1,0:T(8,128)}, u32[]{:S(2)}) copy-start(f32[1536,128]{1,0:T(8,128)} %param.28) | copy-start | bytes 2359300
  7.2 7.5 %copy-start.93 = (s32[1,512]{1,0:T(1,128)S(1)}, s32[1,512]{1,0:T(1,128)}, u32[]{:S(2)}) copy-start(s32[1,512]{1,0:T(1,128)} %param.17) | copy-start | bytes 6148
  7.3 9.0 %copy-start.62 = (bf16[1,256,1024]{2,1,0:T(8,128)(2,1)S(1)}, bf16[1,256,1024]{2,1,0:T(8,128)(2,1)}, u32[]{:S(2)}) copy-start(bf16[1,256,1024]{2,1,0:T(8,128)(2,1)} %param.16) | copy-start | bytes 1572868
  7.3 70.2 %all-gather.3.cloned.1.call-start = ((), (), s32[]{:S(2)}) async-start(), calls=%async_computation.2 | async-start | bytes 3538944 | tf_op jit(solution)/shard_map/all_gather | solution.py:587
  11.5 7.7 %copy-start.94 = (s32[4]{0:T(128)S(1)}, s32[4]{0:T(128)}, u32[]{:S(2)}) copy-start(s32[4]{0:T(128)} %constant.115.clone) | copy-start | bytes 52
  11.5 7.7 %copy-start.95 = (s32[4]{0:T(128)S(1)}, s32[4]{0:T(128)}, u32[]{:S(2)}) copy-start(s32[4]{0:T(128)} %constant.114.clone) | copy-start | bytes 52
  11.6 154.2 %all-gather.5.cloned.1.call-start = ((), (), s32[]{:S(2)}) async-start(), calls=%async_computation.3 | async-start | bytes 5308416 | tf_op jit(solution)/shard_map/all_gather | solution.py:588
  11.8 7.6 %collective-permute-start.2 = (bf16[1,288]{1,0:T(2,128)(2,1)S(1)}, bf16[1,288]{1,0:T(2,128)(2,1)S(1)}, u32[]{:S(2)}, u32[]{:S(2)}) collective-permute-start(bf16[1,288]{1,0:T(2,128)(2,1)S(1)} %pad_maximum_fusion.26), channel_id=1, source_target_pairs={{0,4},{4,0},{8,12},{12,8},{16,20},{20,16},{24,28},{28,24},{1,5},{5... | collective-permute-start | bytes 1736 | tf_op jit(solution)/shard_map/ppermute | solution.py:498
  14.7 11.0 %collective-permute-start.5 = (s32[1,512]{1,0:T(1,128)S(1)}, s32[1,512]{1,0:T(1,128)S(1)}, u32[]{:S(2)}, u32[]{:S(2)}) collective-permute-start(s32[1,512]{1,0:T(1,128)S(1)} %copy-done.93), channel_id=1, source_target_pairs={{0,2},{2,0},{1,3},{3,1},{4,6},{6,4},{5,7},{7,5},{8,10},{10,8},{9,1... | collective-permute-start | bytes 6152 | tf_op jit(solution)/shard_map/ppermute | solution.py:498
  16.2 13.1 %collective-permute-start = (bf16[256,1024]{1,0:T(8,128)(2,1)S(1)}, bf16[256,1024]{1,0:T(8,128)(2,1)S(1)}, u32[]{:S(2)}, u32[]{:S(2)}) collective-permute-start(bf16[256,1024]{1,0:T(8,128)(2,1)S(1)} %bitcast.137), channel_id=1, source_target_pairs={{0,2},{2,0},{1,3},{3,1},{4,6},{6,4},{5,7},{7,5},{8,10},{10,8},{9,1... | collective-permute-start | bytes 1572872 | tf_op jit(solution)/shard_map/ppermute | solution.py:498
  19.1 333.9 %reduce-scatter.5.cloned.1.call-start = ((), (), s32[]{:S(2)}) async-start(), calls=%async_computation.4 | async-start | bytes 5308416 | tf_op jit(solution)/shard_map/reduce_scatter | solution.py:691
  19.4 3.6 collective-permute-start.3
  23.0 9.2 %collective-permute-start.4 = (bf16[4,288]{1,0:T(4,128)(2,1)S(1)}, bf16[4,288]{1,0:T(4,128)(2,1)S(1)}, u32[]{:S(2)}, u32[]{:S(2)}) collective-permute-start(bf16[4,288]{1,0:T(4,128)(2,1)S(1)} %maximum_select_fusion.8), channel_id=1, source_target_pairs={{0,16},{4,20},{8,24},{12,28},{16,0},{20,4},{24,8},{28,12},{1,17},{... | collective-permute-start | bytes 6920 | tf_op jit(solution)/shard_map/ppermute | solution.py:498
  29.3 48.1 %copy-start.66 = (bf16[256,1024]{1,0:T(8,128)(2,1)}, bf16[256,1024]{1,0:T(8,128)(2,1)S(1)}, u32[]{:S(2)}) copy-start(bf16[256,1024]{1,0:T(8,128)(2,1)S(1)} %collective-permute-done) | copy-start | bytes 1572868
  30.5 2.9 collective-permute-start.1
  32.2 76.8 %copy-start.6 = (s32[1024,1]{1,0:T(8,128)}, s32[1024,1]{1,0:T(8,128)S(1)}, u32[]{:S(2)}) copy-start(s32[1024,1]{1,0:T(8,128)S(1)} %reshape.255.column_ref) | copy-start | bytes 12292
  33.3 44.1 %copy-start.53 = (bf16[512,1024]{1,0:T(8,128)(2,1)}, bf16[512,1024]{1,0:T(8,128)(2,1)S(1)}, u32[]{:S(2)}) copy-start(bf16[512,1024]{1,0:T(8,128)(2,1)S(1)} %collective-permute-done.1) | copy-start | bytes 3145732
  33.8 303.4 %copy-start.92 = (f32[1024]{0:T(1024)}, f32[1024]{0:T(1024)S(1)}, u32[]{:S(2)}) copy-start(f32[1024]{0:T(1024)S(1)} %add_rsqrt_fusion.2) | copy-start | bytes 12292
  81.5 27.4 %copy-start.8 = (bf16[1024,256]{1,0:T(8,128)(2,1)}, bf16[1024,256]{1,0:T(8,128)(2,1)S(1)}, u32[]{:S(2)}) copy-start(bf16[1024,256]{1,0:T(8,128)(2,1)S(1)} %slice.400.v_ref) | copy-start | bytes 1572868
  91.9 13.3 %copy-start.39 = (f32[1024,4]{1,0:T(8,128)}, f32[1024,4]{1,0:T(8,128)S(1)}, u32[]{:S(2)}) copy-start(f32[1024,4]{1,0:T(8,128)S(1)} %add_rsqrt_fusion.1) | copy-start | bytes 49156
  109.0 7.4 %copy-start.2 = (bf16[1024,512]{1,0:T(8,128)(2,1)}, bf16[1024,512]{1,0:T(8,128)(2,1)S(1)}, u32[]{:S(2)}) copy-start(bf16[1024,512]{1,0:T(8,128)(2,1)S(1)} %fusion.9.q_ref) | copy-start | bytes 3145732
  119.5 2.7 collective-permute-start.6
  122.6 25.3 %collective-permute-start.7 = (bf16[512,1024]{1,0:T(8,128)(2,1)S(1)}, bf16[512,1024]{1,0:T(8,128)(2,1)S(1)}, u32[]{:S(2)}, u32[]{:S(2)}) collective-permute-start(bf16[512,1024]{1,0:T(8,128)(2,1)S(1)} %fusion.20), channel_id=1, source_target_pairs={{0,2},{2,0},{1,3},{3,1},{4,6},{6,4},{5,7},{7,5},{8,10},{10,8},{9,1... | collective-permute-start | bytes 3145736 | tf_op jit(solution)/shard_map/ppermute | solution.py:498
  150.2 72.7 %copy-start.17 = (f32[512,1024]{1,0:T(8,128)}, f32[512,1024]{1,0:T(8,128)S(1)}, u32[]{:S(2)}) copy-start(f32[512,1024]{1,0:T(8,128)S(1)} %get-tuple-element.73) | copy-start | bytes 6291460
  150.2 15.5 %collective-permute-start.8 = (bf16[512,1024]{1,0:T(8,128)(2,1)}, bf16[512,1024]{1,0:T(8,128)(2,1)}, u32[]{:S(2)}, u32[]{:S(2)}) collective-permute-start(bf16[512,1024]{1,0:T(8,128)(2,1)} %get-tuple-element.72), channel_id=1, source_target_pairs={{0,1},{1,0},{2,3},{3,2},{4,5},{5,4},{6,7},{7,6},{8,9},{9,8},{10,11... | collective-permute-start | bytes 3145736 | tf_op jit(solution)/shard_map/ppermute | solution.py:498
  150.2 14.3 %collective-permute-start.11 = (bf16[256,1024]{1,0:T(8,128)(2,1)S(1)}, bf16[256,1024]{1,0:T(8,128)(2,1)S(1)}, u32[]{:S(2)}, u32[]{:S(2)}) collective-permute-start(bf16[256,1024]{1,0:T(8,128)(2,1)S(1)} %bitcast.147), channel_id=1, source_target_pairs={{0,2},{2,0},{1,3},{3,1},{4,6},{6,4},{5,7},{7,5},{8,10},{10,8},{9,1... | collective-permute-start | bytes 1572872 | tf_op jit(solution)/shard_map/ppermute | solution.py:498
  165.7 6.1 %collective-permute-start.12 = (bf16[512,1024]{1,0:T(8,128)(2,1)}, bf16[512,1024]{1,0:T(8,128)(2,1)}, u32[]{:S(2)}, u32[]{:S(2)}) collective-permute-start(bf16[512,1024]{1,0:T(8,128)(2,1)} %pad_maximum_fusion.15), channel_id=1, source_target_pairs={{0,1},{1,0},{2,3},{3,2},{4,5},{5,4},{6,7},{7,6},{8,9},{9,8},{10,11... | collective-permute-start | bytes 3145736 | tf_op jit(solution)/shard_map/ppermute | solution.py:498
  182.7 12.0 %collective-permute-start.13 = (bf16[512,1024]{1,0:T(8,128)(2,1)}, bf16[512,1024]{1,0:T(8,128)(2,1)S(1)}, u32[]{:S(2)}, u32[]{:S(2)}) collective-permute-start(bf16[512,1024]{1,0:T(8,128)(2,1)} %slice.395), channel_id=1, source_target_pairs={{0,1},{1,0},{2,3},{3,2},{4,5},{5,4},{6,7},{7,6},{8,9},{9,8},{10,11... | collective-permute-start | bytes 3145736 | tf_op jit(solution)/shard_map/ppermute | solution.py:498
  194.6 171.5 %reduce-scatter.7.cloned.1.call-start = ((), (), s32[]{:S(2)}) async-start(), calls=%async_computation.5 | async-start | bytes 3538944
  196.6 25.7 %copy-start.71 = (f32[1024,1024]{1,0:T(8,128)S(1)}, f32[1024,1024]{1,0:T(8,128)}, u32[]{:S(2)}) copy-start(f32[1024,1024]{1,0:T(8,128)} %copy-done.70) | copy-start | bytes 12582916
  196.6 25.4 %collective-permute-start.14 = (bf16[512,1024]{1,0:T(8,128)(2,1)S(1)}, bf16[512,1024]{1,0:T(8,128)(2,1)S(1)}, u32[]{:S(2)}, u32[]{:S(2)}) collective-permute-start(bf16[512,1024]{1,0:T(8,128)(2,1)S(1)} %fusion.21), channel_id=1, source_target_pairs={{0,2},{2,0},{1,3},{3,1},{4,6},{6,4},{5,7},{7,5},{8,10},{10,8},{9,1... | collective-permute-start | bytes 3145736 | tf_op jit(solution)/shard_map/ppermute | solution.py:498
  225.4 2.7 collective-permute-start.15
  285.7 16.9 %collective-permute-start.9 = (bf16[512,1024]{1,0:T(8,128)(2,1)}, bf16[512,1024]{1,0:T(8,128)(2,1)}, u32[]{:S(2)}, u32[]{:S(2)}) collective-permute-start(bf16[512,1024]{1,0:T(8,128)(2,1)} %slice.396), channel_id=1, source_target_pairs={{0,1},{1,0},{2,3},{3,2},{4,5},{5,4},{6,7},{7,6},{8,9},{9,8},{10,11... | collective-permute-start | bytes 3145736 | tf_op jit(solution)/shard_map/ppermute | solution.py:498
  291.8 19.5 %collective-permute-start.16 = (bf16[512,1024]{1,0:T(8,128)(2,1)}, bf16[512,1024]{1,0:T(8,128)(2,1)}, u32[]{:S(2)}, u32[]{:S(2)}) collective-permute-start(bf16[512,1024]{1,0:T(8,128)(2,1)} %slice.394), channel_id=1, source_target_pairs={{0,1},{1,0},{2,3},{3,2},{4,5},{5,4},{6,7},{7,6},{8,9},{9,8},{10,11... | collective-permute-start | bytes 3145736 | tf_op jit(solution)/shard_map/ppermute | solution.py:498
  307.1 33.8 %collective-permute-start.10 = (bf16[256,1024]{1,0:T(8,128)(2,1)}, bf16[256,1024]{1,0:T(8,128)(2,1)}, u32[]{:S(2)}, u32[]{:S(2)}) collective-permute-start(bf16[256,1024]{1,0:T(8,128)(2,1)} %slice.399), channel_id=1, source_target_pairs={{0,2},{2,0},{1,3},{3,1},{4,6},{6,4},{5,7},{7,5},{8,10},{10,8},{9,1... | collective-permute-start | bytes 1572872 | tf_op jit(solution)/shard_map/ppermute | solution.py:498
  313.6 18.9 %copy-start.47 = (f32[512,1024]{1,0:T(8,128)}, f32[512,1024]{1,0:T(8,128)S(1)}, u32[]{:S(2)}) copy-start(f32[512,1024]{1,0:T(8,128)S(1)} %slice_add_fusion) | copy-start | bytes 6291460
  313.7 18.8 %collective-permute-start.17 = (bf16[256,1024]{1,0:T(8,128)(2,1)S(1)}, bf16[256,1024]{1,0:T(8,128)(2,1)S(1)}, u32[]{:S(2)}, u32[]{:S(2)}) collective-permute-start(bf16[256,1024]{1,0:T(8,128)(2,1)S(1)} %slice.398), channel_id=1, source_target_pairs={{0,2},{2,0},{1,3},{3,1},{4,6},{6,4},{5,7},{7,5},{8,10},{10,8},{9,1... | collective-permute-start | bytes 1572872 | tf_op jit(solution)/shard_map/ppermute | solution.py:498
  320.6 20.3 %copy-start.38 = (f32[512,1024]{1,0:T(8,128)S(1)}, f32[512,1024]{1,0:T(8,128)}, u32[]{:S(2)}) copy-start(f32[512,1024]{1,0:T(8,128)} %copy-done.37) | copy-start | bytes 6291460
  334.4 13.9 %copy-start.77 = (bf16[256,1024]{1,0:T(8,128)(2,1)S(1)}, bf16[256,1024]{1,0:T(8,128)(2,1)}, u32[]{:S(2)}) copy-start(bf16[256,1024]{1,0:T(8,128)(2,1)} %copy-done.76) | copy-start | bytes 1572868
  334.4 1.2 collective-permute-start.18
  335.7 3.7 collective-permute-start.19
  337.2 11.1 %copy-start.48 = (f32[512,1024]{1,0:T(8,128)S(1)}, f32[512,1024]{1,0:T(8,128)}, u32[]{:S(2)}) copy-start(f32[512,1024]{1,0:T(8,128)} %copy-done.47) | copy-start | bytes 6291460
  337.2 11.1 %slice-start = ((f32[1024]{0:T(1024)}), f32[256]{0:T(256)S(1)}, s32[]{:S(2)}) async-start(f32[1024]{0:T(1024)} %copy-done.92), calls=%async_computation.6 | async-start | bytes 2048 | tf_op jit(solution)/shard_map/slice | solution.py:686
  339.4 4.1 %collective-permute-start.20 = (f32[2304]{0:T(1024)S(1)}, f32[2304]{0:T(1024)S(1)}, u32[]{:S(2)}, u32[]{:S(2)}) collective-permute-start(f32[2304]{0:T(1024)S(1)} %add.215), channel_id=1, source_target_pairs={{0,4},{4,0},{8,12},{12,8},{16,20},{20,16},{24,28},{28,24},{1,5},{5... | collective-permute-start | bytes 27656 | tf_op jit(solution)/shard_map/ppermute | solution.py:498
  343.5 3.8 collective-permute-start.21
  347.2 4.7 %collective-permute-start.22 = (f32[2304]{0:T(1024)S(1)}, f32[2304]{0:T(1024)S(1)}, u32[]{:S(2)}, u32[]{:S(2)}) collective-permute-start(f32[2304]{0:T(1024)S(1)} %add.217), channel_id=1, source_target_pairs={{0,16},{4,20},{8,24},{12,28},{16,0},{20,4},{24,8},{28,12},{1,17},{... | collective-permute-start | bytes 27656 | tf_op jit(solution)/shard_map/ppermute | solution.py:498
  354.2 27.3 %collective-permute-start.24 = (bf16[64,2304]{1,0:T(8,128)(2,1)S(1)}, bf16[64,2304]{1,0:T(8,128)(2,1)S(1)}, u32[]{:S(2)}, u32[]{:S(2)}) collective-permute-start(bf16[64,2304]{1,0:T(8,128)(2,1)S(1)} %get-tuple-element.97), channel_id=1, source_target_pairs={{0,2},{2,0},{1,3},{3,1},{4,6},{6,4},{5,7},{7,5},{8,10},{10,8},{9,1... | collective-permute-start | bytes 884744 | tf_op jit(solution)/shard_map/ppermute | solution.py:498
  367.6 10.3 %collective-permute-start.23 = (bf16[64,1536]{0,1:T(8,128)(2,1)S(1)}, bf16[64,1536]{0,1:T(8,128)(2,1)S(1)}, u32[]{:S(2)}, u32[]{:S(2)}) collective-permute-start(bf16[64,1536]{0,1:T(8,128)(2,1)S(1)} %copy.95), channel_id=1, source_target_pairs={{0,2},{2,0},{1,3},{3,1},{4,6},{6,4},{5,7},{7,5},{8,10},{10,8},{9,1... | collective-permute-start | bytes 589832 | tf_op jit(solution)/shard_map/ppermute | solution.py:498
  (87 other events, 280.3 us)
Sparse Core Ops, SparseCore 0:
  11.7 65.7 all-gather.2
  79.5 80.0 all-gather.4
  194.7 93.6 reduce-scatter.4
  291.9 74.1 reduce-scatter.6

commit v2 on v0

--- a/solution.py
+++ b/solution.py
@@ -1,6 +1,10 @@
+import functools
+
 import jax
 import jax.numpy as jnp
 from jax import lax
+from jax.experimental import pallas as pl
+from jax.experimental.pallas import tpu as pltpu
 from jax.sharding import PartitionSpec as P
 
 HD = 128
@@ -119,7 +123,7 @@
     return (grad_queries, grad_keys, grad_values)
 
 
-def body(
+def split_body(
     tokens,
     places,
     attn_gain,
@@ -313,6 +317,861 @@
     )
 
 
+NT = (((1,), (1,)), ((), ()))
+TN = (((0,), (0,)), ((), ()))
+NN = (((1,), (0,)), ((), ()))
+SCALE = HD ** (-0.5)
+GAIN_ROWS = 16
+VMEM_LIMIT = 44 * 1024 * 1024
+COST = 2
+
+
+def dot(left, right, dims=NN):
+    return lax.dot_general(left, right, dims, preferred_element_type=jnp.float32)
+
+
+def shape_of(shape, dtype):
+    return jax.ShapeDtypeStruct(shape, dtype)
+
+
+def call(kernel, grid, words, inputs, outputs, scratch, flops):
+
+    def spec(block, index):
+        if index is None:
+            return pl.BlockSpec(block, lambda *ids: (0,) * len(block))
+        return pl.BlockSpec(block, index)
+
+    return pl.pallas_call(
+        kernel,
+        grid_spec=pltpu.PrefetchScalarGridSpec(
+            num_scalar_prefetch=1,
+            grid=(grid,),
+            in_specs=[spec(block, index) for _, block, index in inputs],
+            out_specs=[spec(block, index) for _, _, block, index in outputs],
+            scratch_shapes=scratch,
+        ),
+        out_shape=[shape_of(shape, dtype) for shape, dtype, _, _ in outputs],
+        compiler_params=pltpu.CompilerParams(vmem_limit_bytes=VMEM_LIMIT),
+        cost_estimate=pl.CostEstimate(flops=COST * flops, bytes_accessed=0, transcendentals=0),
+    )(words, *[array for array, _, _ in inputs])
+
+
+def whole(array):
+    return (array, array.shape, None)
+
+
+def sort_runs(block_of, run, *pairs):
+    for index in range(4):
+        source = pl.multiple_of(block_of[index] * run, run)
+        for target, origin in pairs:
+            target[pl.ds(index * run, run), :] = origin[pl.ds(source, run), :]
+
+
+def turn(source):
+    return pltpu.roll(source, HD // 2, 1)
+
+
+def unit_of(raw):
+    factor = lax.rsqrt(jnp.mean(raw * raw, axis=-1, keepdims=True) + EPSILON)
+    return (raw * factor, factor)
+
+
+def raw_scores(keys, query, visible, run):
+    scores = dot(keys, query, NT) * SCALE
+    count = scores.shape[0]
+    last = jnp.where(visible, scores[count - run :], NEGATIVE)
+    if count == run:
+        return last
+    return jnp.concatenate([scores[: count - run], last], axis=0)
+
+
+def place_all(member, groups, refs, target, columns=slice(None), depth=None):
+    for indices, ref in zip(groups, refs):
+        for place, index in enumerate(indices):
+            value = ref[place] if depth is None else ref[place, :depth]
+            size = value.shape[0]
+            start = pl.multiple_of((member ^ index) * size, size)
+            target[pl.ds(start, size), columns] = value
+
+
+def pick(first_ref, second_ref):
+    half = pl.num_programs(0) // 2
+    return jnp.where(pl.program_id(0) < half, first_ref[...], second_ref[...])
+
+
+def project_kernel(groups, member_ref, xa_ref, xb_ref, cos_ref, sin_ref, *refs):
+    pieces, rest = refs[:-7], refs[-7:]
+    normed_ref, q_ref, k_ref, v_ref, raw_ref, weight_ref, gains_ref = rest
+    depth = pieces[0].shape[1] - GAIN_ROWS
+
+    @pl.when(pl.program_id(0) == 0)
+    def _():
+        place_all(member_ref[0], groups, pieces, weight_ref, depth=depth)
+        gains = jnp.zeros(gains_ref.shape, jnp.float32)
+        for piece in pieces:
+            for place in range(piece.shape[0]):
+                gains += piece[place, depth:].astype(jnp.float32)
+        gains_ref[...] = gains
+
+    unit, _ = unit_of(pick(xa_ref, xb_ref).astype(jnp.float32))
+    normed = (unit * gains_ref[0:1, :]).astype(jnp.bfloat16)
+    normed_ref[...] = normed
+    product = dot(normed, weight_ref[...])
+    raw_width = raw_ref.shape[1]
+    raw_ref[...] = product[:, :raw_width]
+    v_ref[...] = product[:, raw_width:].astype(jnp.bfloat16)
+    cosine = cos_ref[...]
+    sine = sin_ref[...]
+    q_heads = q_ref.shape[1] // HD
+    for head in range(raw_width // HD):
+        unit, _ = unit_of(product[:, head * HD : (head + 1) * HD])
+        target, place, row = (q_ref, head, 2) if head < q_heads else (k_ref, head - q_heads, 3)
+        normed = unit * gains_ref[row : row + 1, :HD]
+        rotated = normed * cosine + turn(normed) * sine
+        target[:, place * HD : (place + 1) * HD] = rotated.astype(jnp.bfloat16)
+
+
+def project(member, x_first, x_second, groups, pieces, cosine, sine, q_width, k_width):
+    rows = cosine.shape[0]
+    width = x_first.shape[1]
+    block = rows // 4
+    total = q_width + 2 * k_width
+    bf16, f32 = jnp.bfloat16, jnp.float32
+
+    def by_rows(i, member):
+        return (i, 0)
+
+    return call(
+        functools.partial(project_kernel, groups),
+        4,
+        member,
+        [
+            (x_first, (block, width), first_half),
+            (x_second, (block, width), second_half),
+            (cosine, (block, HD), by_rows),
+            (sine, (block, HD), by_rows),
+        ]
+        + [whole(piece) for piece in pieces],
+        [
+            ((rows, width), bf16, (block, width), by_rows),
+            ((rows, q_width), bf16, (block, q_width), by_rows),
+            ((rows, k_width), bf16, (block, k_width), by_rows),
+            ((rows, k_width), bf16, (block, k_width), by_rows),
+            ((rows, q_width + k_width), f32, (block, q_width + k_width), by_rows),
+            ((width, total), bf16, (width, total), None),
+            ((GAIN_ROWS, width), f32, (GAIN_ROWS, width), None),
+        ],
+        [],
+        2 * rows * width * total,
+    )
+
+
+def forward_kernel(
+    block_of, q_ref, k_ref, v_ref, column_ref, row_ref, mixed_ref, lse_ref, keys, values, columns
+):
+    run = q_ref.shape[0] // 4
+    sort_runs(block_of, run, (keys, k_ref), (values, v_ref), (columns, column_ref))
+    for index in range(4):
+        count = run * (index + 1)
+        rows = pl.ds(pl.multiple_of(block_of[index] * run, run), run)
+        visible = columns[pl.ds(count - run, run), :] <= row_ref[:, rows]
+        for head in range(q_ref.shape[1] // HD):
+            lanes = pl.ds(head * HD, HD)
+            scores = raw_scores(keys[:count], q_ref[rows, lanes], visible, run)
+            row_max = jnp.max(scores, axis=0, keepdims=True)
+            raised = jnp.exp(scores - row_max)
+            row_total = jnp.sum(raised, axis=0, keepdims=True)
+            probs = (raised * (1.0 / row_total)).astype(jnp.bfloat16)
+            mixed_ref[rows, lanes] = dot(probs, values[:count], TN).astype(jnp.bfloat16)
+            lse_ref[pl.ds(head, 1), rows] = row_max + jnp.log(row_total)
+
+
+def by_group(group, order):
+    return (0, group)
+
+
+def by_lead(group, order):
+    return (group, 0, 0)
+
+
+def attend(block_of, queries, keys, values, column, row):
+    rows, width = keys.shape
+    groups = width // HD
+    pair = queries.shape[1] // groups
+    return call(
+        forward_kernel,
+        groups,
+        block_of,
+        [
+            (queries, (rows, pair), by_group),
+            (keys, (rows, HD), by_group),
+            (values, (rows, HD), by_group),
+            whole(column),
+            whole(row),
+        ],
+        [
+            (queries.shape, jnp.bfloat16, (rows, pair), by_group),
+            ((groups, pair // HD, rows), jnp.float32, (None, pair // HD, rows), by_lead),
+        ],
+        [
+            pltpu.VMEM((rows, HD), jnp.bfloat16),
+            pltpu.VMEM((rows, HD), jnp.bfloat16),
+            pltpu.VMEM((rows, 1), jnp.int32),
+        ],
+        3 * rows * rows * queries.shape[1],
+    )
+
+
+def first_half(i, member):
+    return (jnp.minimum(i, 1), 0)
+
+
+def second_half(i, member):
+    return (jnp.maximum(i - 2, 0), 0)
+
+
+def store_halves(product, kept_ref, sent_ref):
+    half = pl.num_programs(0) // 2
+
+    @pl.when(pl.program_id(0) < half)
+    def _():
+        kept_ref[...] = product
+
+    @pl.when(pl.program_id(0) >= half)
+    def _():
+        sent_ref[...] = product.astype(jnp.bfloat16)
+
+
+def halves_out(rows, block, width):
+    return [
+        ((rows // 2, width), jnp.float32, (block, width), first_half),
+        ((rows // 2, width), jnp.bfloat16, (block, width), second_half),
+    ]
+
+
+def out_kernel(groups, member_ref, mixed_ref, *refs):
+    pieces, (kept_ref, sent_ref, weight_ref) = refs[:-3], refs[-3:]
+
+    @pl.when(pl.program_id(0) == 0)
+    def _():
+        place_all(member_ref[0], groups, pieces, weight_ref)
+
+    store_halves(dot(mixed_ref[...], weight_ref[...], NT), kept_ref, sent_ref)
+
+
+def project_out(member, mixed, groups, pieces):
+    rows, depth = mixed.shape
+    block = rows // 4
+    width = pieces[0].shape[1] * sum(piece.shape[0] for piece in pieces)
+    return call(
+        functools.partial(out_kernel, groups),
+        4,
+        member,
+        [(mixed, (block, depth), lambda i, member: (i, 0))] + [whole(piece) for piece in pieces],
+        halves_out(rows, block, width)
+        + [((width, depth), jnp.bfloat16, (width, depth), None)],
+        [],
+        2 * rows * width * depth,
+    )
+
+
+def back_kernel(starts, member_ref, xa_ref, xb_ref, *refs):
+    grad_refs, (weight_ref, kept_ref, sent_ref, gain_ref) = refs[:-4], refs[-4:]
+    product = None
+    for start, grad_ref in zip(starts, grad_refs):
+        term = dot(grad_ref[...], weight_ref[:, start : start + grad_ref.shape[1]], NT)
+        product = term if product is None else product + term
+    unit, _ = unit_of(pick(xa_ref, xb_ref).astype(jnp.float32))
+
+    @pl.when(pl.program_id(0) == 0)
+    def _():
+        gain_ref[...] = jnp.zeros_like(gain_ref)
+
+    gain_ref[...] += jnp.sum(product * unit, axis=0, keepdims=True)
+    store_halves(product, kept_ref, sent_ref)
+
+
+def project_back(member, x_first, x_second, starts, grads, weight):
+    rows = grads[0].shape[0]
+    block = rows // 4
+    width, total = weight.shape
+    return call(
+        functools.partial(back_kernel, starts),
+        4,
+        member,
+        [
+            (x_first, (block, width), first_half),
+            (x_second, (block, width), second_half),
+        ]
+        + [(grad, (block, grad.shape[1]), lambda i, member: (i, 0)) for grad in grads]
+        + [whole(weight)],
+        halves_out(rows, block, width) + [((1, width), jnp.float32, (1, width), None)],
+        [],
+        2 * rows * width * total,
+    )
+
+
+def mlp_kernel(member_ref, xa_ref, xb_ref, ga_ref, gb_ref, gate_up, down_ref, *rest):
+    bf16 = jnp.bfloat16
+    hidden_ref, grad_ref, kept_ref, sent_ref = rest
+    width = down_ref.shape[1]
+    x = pick(xa_ref, xb_ref)
+    product = dot(x, gate_up[...])
+    grad_hidden = dot(pick(ga_ref, gb_ref), down_ref[...])
+    gate = product[:, :width]
+    up = product[:, width:]
+    sigmoid = jax.nn.sigmoid(gate)
+    silu = gate * sigmoid
+    hidden_ref[...] = (silu * up).astype(bf16)
+    grad_gate = (grad_hidden * up * sigmoid * (1.0 + gate * (1.0 - sigmoid))).astype(bf16)
+    grad_up = (grad_hidden * silu).astype(bf16)
+    grad_ref[:, :width] = grad_gate
+    grad_ref[:, width:] = grad_up
+    grad_x = dot(grad_gate, gate_up[:, :width], NT) + dot(grad_up, gate_up[:, width:], NT)
+    store_halves(grad_x, kept_ref, sent_ref)
+
+
+def third_quarter(i, member):
+    return (2 + jnp.minimum(i, 1), 0)
+
+
+def fourth_quarter(i, member):
+    return (jnp.maximum(i, 2), 0)
+
+
+def feed(member, x_first, x_second, own_half, core_half, weight):
+    rows, width = own_half.shape
+    hidden_width = weight.shape[1] // 3
+    block = rows // 4
+    bf16 = jnp.bfloat16
+
+    def by_rows(i, member):
+        return (i, 0)
+
+    return call(
+        mlp_kernel,
+        4,
+        member,
+        [
+            (x_first, (block, width), first_half),
+            (x_second, (block, width), second_half),
+            (own_half, (block, width), third_quarter),
+            (core_half, (block, width), fourth_quarter),
+            (weight, (width, 2 * hidden_width), lambda i, member: (0, 0)),
+            (weight, (width, hidden_width), lambda i, member: (0, 2)),
+        ],
+        [
+            ((rows, hidden_width), bf16, (block, hidden_width), by_rows),
+            ((rows, 2 * hidden_width), bf16, (block, 2 * hidden_width), by_rows),
+        ]
+        + halves_out(rows, block, width),
+        [],
+        10 * rows * width * hidden_width,
+    )
+
+
+def mlp_grad_kernel(member_ref, xa_ref, xb_ref, ga_ref, gb_ref, grad_ref, hidden_ref, out_ref):
+    half = xa_ref.shape[0]
+    split = grad_ref.shape[1]
+    product = dot(xa_ref[...], grad_ref[:half, :], TN) + dot(xb_ref[...], grad_ref[half:, :], TN)
+    out_ref[:, :split] = product.astype(jnp.bfloat16)
+    product = dot(ga_ref[...], hidden_ref[:half, :], TN) + dot(gb_ref[...], hidden_ref[half:, :], TN)
+    out_ref[:, split:] = product.astype(jnp.bfloat16)
+
+
+def mlp_grads(member, x_first, x_second, own_half, core_half, grad_gate_up, hidden):
+    rows, width = own_half.shape
+    block = width // 4
+    total = grad_gate_up.shape[1] + hidden.shape[1]
+
+    def by_columns(i, member):
+        return (0, i)
+
+    def low_columns(i, member):
+        return (1, i)
+
+    return call(
+        mlp_grad_kernel,
+        4,
+        member,
+        [
+            (x_first, (rows // 2, block), by_columns),
+            (x_second, (rows // 2, block), by_columns),
+            (own_half, (rows // 2, block), low_columns),
+            (core_half, (rows // 2, block), low_columns),
+            whole(grad_gate_up),
+            whole(hidden),
+        ],
+        [((width, total), jnp.bfloat16, (block, total), lambda i, member: (i, 0))],
+        [],
+        2 * rows * width * total,
+    )[0]
+
+
+def weight_grad_kernel(lefts, member_ref, *refs):
+    left_refs, right_refs, rest = refs[:lefts], refs[lefts:-3], refs[-3:]
+    kept_ref, sent_ref, product = rest
+    half = kept_ref.shape[0]
+    start = 0
+    for right_ref in right_refs:
+        stop = start + right_ref.shape[1]
+        total = None
+        row = 0
+        for left_ref in left_refs:
+            count = left_ref.shape[0]
+            term = dot(left_ref[...], right_ref[row : row + count, :], TN)
+            total = term if total is None else total + term
+            row += count
+        product[:, start:stop] = total.astype(jnp.bfloat16)
+        start = stop
+    near = member_ref[0] % 2
+    kept_ref[...] = product[pl.ds(pl.multiple_of(near * half, half), half), :]
+    sent_ref[...] = product[pl.ds(pl.multiple_of((1 - near) * half, half), half), :]
+
+
+def weight_grad(member, dp_size, lefts, rights, quarter=0):
+    width = lefts[0].shape[1]
+    rows = rights[0].shape[0]
+    each = rows // len(lefts)
+    pairs = dp_size // 2
+    half = width // dp_size
+    total = sum(right.shape[1] for right in rights)
+
+    def by_lead(i, member):
+        return (i, 0, 0)
+
+    bits = pairs.bit_length() - 1
+
+    def by_member(i, member):
+        turned = sum(((i >> bit) & 1) << (bits - 1 - bit) for bit in range(bits))
+        return (quarter, (member[0] // 2) ^ turned)
+
+    result = ((pairs, half, total), jnp.bfloat16, (None, half, total), by_lead)
+    return call(
+        functools.partial(weight_grad_kernel, len(lefts)),
+        pairs,
+        member,
+        [(left, (each, 2 * half), by_member) for left in lefts]
+        + [whole(right) for right in rights],
+        [result, result],
+        [pltpu.VMEM((2 * half, total), jnp.bfloat16)],
+        2 * rows * width * total,
+    )
+
+
+def norm_rope_back(grad, raw, cosine, sine, gain):
+    grad_normed = grad * cosine - turn(grad) * sine
+    unit, factor = unit_of(raw)
+    gain_part = jnp.sum(grad_normed * unit, axis=0, keepdims=True)
+    grad_unit = grad_normed * gain
+    projected = jnp.mean(grad_unit * unit, axis=-1, keepdims=True)
+    return ((factor * (grad_unit - unit * projected)).astype(jnp.bfloat16), gain_part)
+
+
+def backward_kernel(
+    block_of,
+    q_ref,
+    k_ref,
+    v_ref,
+    branch_a_ref,
+    branch_b_ref,
+    out_weight_ref,
+    lse_ref,
+    column_ref,
+    row_ref,
+    raw_q_ref,
+    raw_k_ref,
+    cos_ref,
+    sin_ref,
+    gains_ref,
+    dq_ref,
+    dk_ref,
+    dv_ref,
+    q_part_ref,
+    k_part_ref,
+    keys,
+    values,
+    columns,
+    key_sum,
+    value_sum,
+    grad_mixed,
+):
+    run = q_ref.shape[0] // 4
+    sort_runs(block_of, run, (keys, k_ref), (values, v_ref), (columns, column_ref))
+    key_sum[...] = jnp.zeros_like(key_sum)
+    value_sum[...] = jnp.zeros_like(value_sum)
+    half = branch_a_ref.shape[0]
+    grad_mixed[:half, :] = dot(branch_a_ref[...], out_weight_ref[...]).astype(jnp.bfloat16)
+    grad_mixed[half:, :] = dot(branch_b_ref[...], out_weight_ref[...]).astype(jnp.bfloat16)
+    q_part = jnp.zeros((1, HD), jnp.float32)
+    k_part = jnp.zeros((1, HD), jnp.float32)
+    q_gain = gains_ref[2:3, :HD]
+    k_gain = gains_ref[3:4, :HD]
+    for index in range(4):
+        count = run * (index + 1)
+        rows = pl.ds(pl.multiple_of(block_of[index] * run, run), run)
+        visible = columns[pl.ds(count - run, run), :] <= row_ref[:, rows]
+        for head in range(q_ref.shape[1] // HD):
+            lanes = pl.ds(head * HD, HD)
+            query = q_ref[rows, lanes]
+            grad = grad_mixed[rows, lanes]
+            scores = raw_scores(keys[:count], query, visible, run)
+            probs = jnp.exp(scores - lse_ref[pl.ds(head, 1), rows])
+            grad_probs = dot(values[:count], grad, NT)
+            delta = jnp.sum(probs * grad_probs, axis=0, keepdims=True)
+            grad_scores = (probs * (grad_probs - delta)).astype(jnp.bfloat16)
+            value_sum[:count, :] += dot(probs.astype(jnp.bfloat16), grad)
+            key_sum[:count, :] += dot(grad_scores, query)
+            grad_query = dot(grad_scores, keys[:count], TN) * SCALE
+            dq_ref[rows, lanes], part = norm_rope_back(
+                grad_query, raw_q_ref[rows, lanes], cos_ref[rows, :], sin_ref[rows, :], q_gain
+            )
+            q_part += part
+    for index in range(4):
+        rows = pl.ds(pl.multiple_of(block_of[index] * run, run), run)
+        sorted_rows = pl.ds(index * run, run)
+        dk_ref[rows, :], part = norm_rope_back(
+            key_sum[sorted_rows, :] * SCALE,
+            raw_k_ref[rows, :],
+            cos_ref[rows, :],
+            sin_ref[rows, :],
+            k_gain,
+        )
+        k_part += part
+        dv_ref[rows, :] = value_sum[sorted_rows, :].astype(jnp.bfloat16)
+    q_part_ref[...] = q_part
+    k_part_ref[...] = k_part
+
+
+def attend_back(
+    group, block_of, queries, keys, values, branches, out_weight, lse, column, row, raw, cosine, sine, gains
+):
+    rows, width = keys.shape
+    groups = width // HD
+    pair = queries.shape[1] // groups
+    first_key = queries.shape[1] // HD
+    depth = out_weight.shape[0]
+    bf16, f32 = jnp.bfloat16, jnp.float32
+    part = ((1, HD), f32, (1, HD), None)
+
+    def this_group(i, order):
+        return (0, group)
+
+    return call(
+        backward_kernel,
+        1,
+        block_of,
+        [
+            (queries, (rows, pair), this_group),
+            (keys, (rows, HD), this_group),
+            (values, (rows, HD), this_group),
+            whole(branches[0]),
+            whole(branches[1]),
+            (out_weight, (depth, pair), this_group),
+            (lse, (None, pair // HD, rows), lambda i, order: (group, 0, 0)),
+            whole(column),
+            whole(row),
+            (raw, (rows, pair), this_group),
+            (raw, (rows, HD), lambda i, order: (0, first_key + group)),
+            whole(cosine),
+            whole(sine),
+            whole(gains),
+        ],
+        [
+            ((rows, pair), bf16, (rows, pair), None),
+            ((rows, HD), bf16, (rows, HD), None),
+            ((rows, HD), bf16, (rows, HD), None),
+            part,
+            part,
+        ],
+        [
+            pltpu.VMEM((rows, HD), bf16),
+            pltpu.VMEM((rows, HD), bf16),
+            pltpu.VMEM((rows, 1), jnp.int32),
+            pltpu.VMEM((rows, HD), f32),
+            pltpu.VMEM((rows, HD), f32),
+            pltpu.VMEM((rows, pair), bf16),
+        ],
+        3 * rows * rows * queries.shape[1],
+    )
+
+
+def swap(source, axis, size, bit=1):
+    return lax.ppermute(source, axis, [(i, i ^ bit) for i in range(size)])
+
+
+def after(source, *events):
+    return lax.optimization_barrier((source, events))[0]
+
+
+def group_body(
+    dp_size,
+    tokens,
+    places,
+    attn_gain,
+    w_query,
+    w_key,
+    w_value,
+    q_gain,
+    k_gain,
+    w_out,
+    mlp_gain,
+    w_gate,
+    w_up,
+    w_down,
+    cotangent,
+):
+    bf16, f32 = jnp.bfloat16, jnp.float32
+    run, width = tokens.shape[1:]
+    side = lax.axis_index("ctx")
+    core = lax.axis_index("tensor")
+    member = lax.axis_index("dp")
+    word = member[None]
+    q_width = w_query.shape[1] // 2
+    k_width = w_key.shape[1] // 2
+    hidden_width = w_gate.shape[1] // 2
+    z_bits = [1 << bit for bit in range(1, dp_size.bit_length() - 1)]
+    near_steps = list(range(2, dp_size, 2))
+    groups = [[0], near_steps, [1], [step ^ 1 for step in near_steps]]
+
+    def over_core(source):
+        return swap(source, "tensor", 2)
+
+    def over_ctx(source):
+        return swap(source, "ctx", 2)
+
+    def over_dp(source, bit):
+        return swap(source, "dp", dp_size, bit)
+
+    def over_z(shard):
+        return [over_dp(shard, step) for step in near_steps]
+
+    def mine(source, axis):
+        size = source.shape[axis] // 2
+        return lax.dynamic_slice_in_dim(source, side * size, size, axis).astype(bf16)
+
+    def sum_small(source):
+        source = source + over_core(source)
+        source = source + over_ctx(source)
+        bit = 1
+        while bit < dp_size:
+            source = source + over_dp(source, bit)
+            bit *= 2
+        return source
+
+    gain_rows = jnp.zeros((GAIN_ROWS, width), bf16)
+    for row, gain in enumerate((attn_gain, mlp_gain, q_gain, k_gain)):
+        gain_rows = lax.dynamic_update_slice(
+            gain_rows, gain.astype(bf16)[None], (row, member * gain.shape[0])
+        )
+    qkv_shard = jnp.concatenate([mine(w_query, 1), mine(w_key, 1), mine(w_value, 1)], axis=1)
+    qkv_shard = jnp.concatenate([qkv_shard, gain_rows], axis=0)
+    depth = qkv_shard.shape[0] - GAIN_ROWS
+    out_shard = mine(w_out, 0).T
+    mlp_shard = jnp.concatenate([mine(w_gate, 1), mine(w_up, 1), mine(w_down, 0).T], axis=1)
+
+    place_count = places.shape[1]
+    digits = jnp.zeros((GAIN_ROWS, width), bf16)
+    for row, digit in enumerate((places // 128, places % 128)):
+        digits = lax.dynamic_update_slice(digits, digit.astype(bf16), (row, 0))
+    message = jnp.concatenate([tokens[0], cotangent[0], digits], axis=0)
+    qkv_near, qkv_far, message = lax.optimization_barrier(
+        (over_z(qkv_shard), over_dp(qkv_shard, 1), over_ctx(message))
+    )
+    qkv_near = jnp.stack(qkv_near)
+    qkv_far_rest = over_dp(qkv_near, 1)
+    mlp_weight = lax.all_gather(after(mlp_shard, qkv_near), "dp", axis=0, tiled=True)
+    out_near = over_z(after(out_shard, qkv_near))
+    own_half = jnp.concatenate(
+        [tokens[0], message[:run], cotangent[0], message[run : 2 * run]], axis=0
+    )
+    core_half = over_core(own_half)
+    half = 2 * run
+    digits = message[2 * run : 2 * run + 2, :place_count].astype(jnp.int32)
+    other_places = (digits[0] * 128 + digits[1]).reshape(2, run)
+    own_places = places[0].reshape(2, run)
+    place_blocks = jnp.stack([own_places, other_places], axis=1)
+    place_blocks = jnp.where(core == 0, place_blocks, place_blocks[::-1]).reshape(-1)
+    place_column = place_blocks[:, None]
+    place_row = place_blocks[None, :]
+    home_side = jnp.array([0, 1, 1, 0], jnp.int32)
+    home_core = jnp.array([0, 0, 1, 1], jnp.int32)
+    block_of = (home_core ^ core) * 2 + (home_side ^ side)
+    cosine, sine_table = (table[:, 0] for table in rope_tables(place_blocks))
+    sine_table = sine_table * jnp.where(jnp.arange(HD) < HD // 2, -1.0, 1.0).astype(f32)
+    own_half, core_half, cosine, sine_table, place_column, block_of = lax.optimization_barrier(
+        (own_half, core_half, cosine, sine_table, place_column, block_of)
+    )
+    normed_one, queries, key_rows, value_rows, raw, qkv_weight, gains = project(
+        word,
+        own_half,
+        core_half,
+        groups,
+        [qkv_shard[None], qkv_near, qkv_far[None], qkv_far_rest],
+        cosine,
+        sine_table,
+        q_width,
+        k_width,
+    )
+
+    out_near = jnp.stack([out_shard] + out_near)
+    out_far = over_dp(out_near, 1)
+    mixed, lse_rows = attend(block_of, queries, key_rows, value_rows, place_column, place_row)
+    orders = [[0] + near_steps, [1] + [step ^ 1 for step in near_steps]]
+    out_kept, out_sent, out_weight = project_out(word, mixed, orders, [out_near, out_far])
+
+    def ctx_sum(summed):
+        sent = summed.astype(bf16)
+        other = over_ctx(sent)
+        return sent, summed, other[run:], other[:run]
+
+    source = own_half[:half].astype(f32)
+    _, summed, first, second = ctx_sum(out_kept + over_core(out_sent).astype(f32))
+    middle = source + summed + jnp.concatenate([first, second], axis=0).astype(f32)
+    gain_two = gains[1]
+    normed_two, unit_two, factor_two = norm_forward(middle, gain_two)
+    normed_two = normed_two.astype(bf16)
+    normed_other = over_core(normed_two)
+    hidden, grad_gate_up, grad_kept, grad_sent = feed(
+        word, normed_two, normed_other, own_half, core_half, mlp_weight
+    )
+
+    def summed_x(pair, *events):
+        kept, sent = pair
+        return kept.astype(f32) + over_dp(after(sent, *events), 1).astype(f32)
+
+    def summed_z(summed, bit):
+        count = summed.shape[0] // 2
+        return summed[:count] + over_dp(summed[count:].astype(bf16), bit).astype(f32)
+
+    def halves(block):
+        size = block.shape[0] // 2
+        kept = lax.dynamic_slice_in_dim(block, side * size, size, 0)
+        sent = lax.dynamic_slice_in_dim(block, (1 - side) * size, size, 0)
+        return kept, sent
+
+    def joined(kept, other):
+        return jnp.where(
+            side == 0,
+            jnp.concatenate([kept, other], axis=1),
+            jnp.concatenate([other, kept], axis=1),
+        )
+
+    def grad_of(lefts, rights, quarter=0):
+        return weight_grad(word, dp_size, lefts, rights, quarter)
+
+    sent, summed, first, second = ctx_sum(grad_kept + over_core(grad_sent).astype(f32))
+    hidden, grad_gate_up = lax.optimization_barrier((hidden, grad_gate_up, sent))[:2]
+    mlp_grad = mlp_grads(
+        word, normed_two, normed_other, own_half, core_half, grad_gate_up, hidden
+    )
+    mlp_block = lax.psum_scatter(mlp_grad, "dp", scatter_dimension=0, tiled=True)
+    mlp_part = dot(after(hidden, mlp_grad), mlp_weight[:, 2 * hidden_width :], NT)
+    mlp_part = mlp_part[:half] + over_core(mlp_part[half:].astype(bf16)).astype(f32)
+    first, second = after((first, second), mlp_part)
+    grad_normed_two = summed + jnp.concatenate([first, second], axis=0).astype(f32)
+    grad_source_two, _ = norm_backward(grad_normed_two, unit_two, factor_two, gain_two)
+    grad_gain_two = jnp.sum(grad_normed_two[:run] * unit_two[:run], axis=0)
+    grad_middle = own_half[half:].astype(f32) + grad_source_two
+    branch = grad_middle.astype(bf16)
+    other_part = over_ctx(after(mlp_part[run:].astype(bf16), branch)).astype(f32)
+    layer_out = middle[:run] + mlp_part[:run] + other_part
+    branches = [branch, over_core(branch)]
+    out_pair = grad_of(branches, [mixed])
+
+    def back(group, *events):
+        return attend_back(
+            group,
+            block_of,
+            after(queries, *events),
+            key_rows,
+            value_rows,
+            branches,
+            out_weight,
+            lse_rows,
+            place_column,
+            place_row,
+            raw,
+            cosine,
+            sine_table,
+            gains,
+        )
+
+    first_back = back(0, out_pair)
+    out_sum = summed_x(out_pair)
+    first_pair = grad_of([normed_one], first_back[:3])
+    second_back = back(1, first_pair, out_sum, other_part)
+    first_sum = summed_x(first_pair)
+    second_pair = grad_of([normed_one], second_back[:3])
+    second_sum = summed_x(second_pair)
+    q_half, k_half = q_width // 2, k_width // 2
+    starts = [0, q_half, q_width, q_width + k_half, q_width + k_width, q_width + k_width + k_half]
+    back_grads = [grads[part] for part in range(3) for grads in (first_back, second_back)]
+    early_sum = jnp.concatenate([out_sum, first_sum], axis=2)
+    back_grads[0] = after(back_grads[0], second_pair, early_sum)
+    one_kept, one_sent, grad_gain_one = project_back(
+        word, own_half, core_half, starts, back_grads, qkv_weight
+    )
+    one_sum = one_kept + over_core(one_sent).astype(f32)
+    one_other = over_ctx(one_sum[run:].astype(bf16)).astype(f32)
+    grad_normed_one = one_sum[:run] + one_other
+    _, unit_one, factor_one = norm_forward(tokens[0].astype(f32), gains[0])
+    grad_source_one, _ = norm_backward(grad_normed_one, unit_one, factor_one, gains[0])
+    grad_tokens = grad_middle[:run] + grad_source_one
+    gain_grads = sum_small(
+        jnp.concatenate(
+            [
+                grad_gain_one[0],
+                grad_gain_two,
+                (first_back[3] + second_back[3])[0],
+                (first_back[4] + second_back[4])[0],
+            ]
+        )
+    )
+
+    def finished(blocks):
+        kept, sent = halves(jnp.concatenate(blocks, axis=1))
+        return kept, over_ctx(sent)
+
+    early_sum = summed_z(early_sum, z_bits[0])
+    late_sum = summed_z(second_sum, z_bits[0])
+    attn_sum = summed_z(jnp.concatenate([early_sum, late_sum], axis=2), z_bits[1])
+    attn_pair = finished([after(attn_sum[0], grad_tokens, gain_grads)])
+    mlp_pair = finished([mlp_block])
+
+    def part(pair, *columns):
+        kept, other = (
+            jnp.concatenate([block[:, start : start + size] for start, size in columns], axis=1)
+            for block in pair
+        )
+        return joined(kept.astype(f32), other.astype(f32))
+
+    start = q_width
+    other_start = start + q_half + 2 * k_half
+    return (
+        layer_out[None],
+        grad_tokens[None],
+        gain_grads[:width],
+        part(attn_pair, (start, q_half), (other_start, q_half)),
+        part(attn_pair, (start + q_half, k_half), (other_start + q_half, k_half)),
+        part(attn_pair, (start + q_half + k_half, k_half), (other_start + q_half + k_half, k_half)),
+        gain_grads[2 * width : 2 * width + HD],
+        gain_grads[2 * width + HD :],
+        part(attn_pair, (0, q_width)).T,
+        gain_grads[width : 2 * width],
+        part(mlp_pair, (0, hidden_width)),
+        part(mlp_pair, (hidden_width, hidden_width)),
+        part(mlp_pair, (2 * hidden_width, hidden_width)).T,
+    )
+
+
+def plan(mesh):
+    sizes = dict(mesh.shape)
+    if sizes["ctx"] == 2 and sizes["tensor"] == 2 and sizes["dp"] == 8:
+        return functools.partial(group_body, sizes["dp"])
+    return split_body
+
+
 def solution(mesh):
     in_specs = (
         P("dp", ("ctx", "tensor"), None),
@@ -345,4 +1204,4 @@
         P(("dp", "ctx"), "tensor"),
         P("tensor", ("dp", "ctx")),
     )
-    return jax.shard_map(body, mesh=mesh, in_specs=in_specs, out_specs=out_specs, check_vma=False)
+    return jax.shard_map(plan(mesh), mesh=mesh, in_specs=in_specs, out_specs=out_specs, check_vma=False)

time: 1510 us -> 366 us (0.24)
  waiting for transfers between devices: 1090 us -> 150 us
  matrix products: 145 us -> 5.75 us
  blocking collectives: 102 us -> 0 us
  Pallas kernels: 0 us -> 79.5 us
  local copies, waits for them, and re-layouts: 72.9 us -> 30.8 us
  starting transfers between devices: 1.91 us -> 42.4 us
  other arithmetic: 70.1 us -> 36.7 us
    reduce_scatter x12 -> x1, waiting for transfers between devices: 747 us -> 0.02 us  [group_body(): lax.psum_scatter(mlp_grad, 'dp', scatter_dimension=0, tiled=True)]
    all_gather x13 -> x1, waiting for transfers between devices: 344 us -> 0.01 us  [group_body(): lax.all_gather(after(mlp_shard, qkv_near), 'dp', axis=0, tiled=True)]
    ppermute x0 -> x34, waiting for transfers between devices: none -> 150 us  [swap(): return lax.ppermute(source, axis, [(i, i ^ bit) for i in range(size)])]
    dot_general x49 -> x1, matrix products: 145 us -> 5.75 us  [dot(): lax.dot_general(left, right, dims, preferred_element_type=jnp.float32)]
    pallas_call x0 -> x11, Pallas kernels: none -> 79.5 us  [call(): pl.pallas_call(kernel, grid_spec=pltpu.PrefetchScalarGridSpec(num_scalar_...]
    all_gather x3 -> x0, blocking collectives: 44.3 us -> none  [the longest x1 22.1 us: body(): lax.all_gather(attn_gain.astype(jnp.bfloat16), 'dp', axis=0, tiled=True)]
    ppermute x0 -> x34, starting transfers between devices: none -> 42.3 us  [swap(): return lax.ppermute(source, axis, [(i, i ^ bit) for i in range(size)])]
    psum x1 -> x0, blocking collectives: 40.4 us -> none  [body(): lax.psum((grad_gain_one, grad_q_part, grad_k_part, grad_gain_two), ('dp',...]
  transfers between devices with their start and end apart: 25 -> 36, of which waited for: 21 -> 19; matrix products, arithmetic and copies ran while one was open for 11% -> 11% of each run, Pallas kernels for 0% -> 15%
where the time goes in v2:
time: 366 us; the launch traced here: 361 us
  waiting for transfers between devices  150 us (41%)
  Pallas kernels  79.5 us (22%)
  starting transfers between devices  42.4 us (12%)
  other arithmetic  36.7 us (10%)
  local copies, waits for them, and re-layouts  30.8 us (8%)
  between operations  15.5 us (4%)
  matrix products  5.75 us (2%)
    ppermute x34, waiting for transfers between devices, swap(): return lax.ppermute(source, axis, [(i, i ^ bit) for i in range(size)])  150 us
    pallas_call x11, Pallas kernels, call(): pl.pallas_call(kernel, grid_spec=pltpu.PrefetchScalarGridSpec(num_scalar_...  79.5 us
    ppermute x34, starting transfers between devices, swap(): return lax.ppermute(source, axis, [(i, i ^ bit) for i in range(size)])  42.3 us
    unnamed x115, local copies, waits for them, and re-layouts  15 us
  transfers between devices with their start and end apart: 36, of which 19 were waited for; matrix products, arithmetic and copies ran while one was open for 11% of the time, Pallas kernels for 15%

profile of v2, /device:TPU:0, one launch (start us, length us, event | category | flops | bytes accessed | tf_op | source)
XLA Modules:
  0.0 360.6 jit_solution(491055393457093029)
XLA Ops:
  10.3 3.0 collective-permute-start.4
  16.2 1.9 collective-permute-start
  18.1 2.6 collective-permute-start.1
  20.7 1.7 collective-permute-start.3
  24.6 5.6 %collective-permute-done = bf16[144,1024]{1,0:T(8,128)(2,1)S(1)} collective-permute-done((bf16[144,1024]{1,0:T(8,128)(2,1)S(1)}, bf16[144,1024]{1,0:T(8,128)(2,1)S(1)}, u32[]{:S(2)}, u32[]{:S(2)}) %collective-permute-start) | collective-permute-done | bytes 294944 | tf_op jit(solution)/shard_map/ppermute | solution.py:900
  30.2 11.5 %collective-permute-done.1 = bf16[144,1024]{1,0:T(8,128)(2,1)} collective-permute-done((bf16[144,1024]{1,0:T(8,128)(2,1)S(1)}, bf16[144,1024]{1,0:T(8,128)(2,1)}, u32[]{:S(2)}, u32[]{:S(2)}) %collective-permute-start.1) | collective-permute-done | bytes 294944 | tf_op jit(solution)/shard_map/ppermute | solution.py:900
  41.7 2.3 pad_maximum_fusion.3.refs_1_
  47.7 5.2 %collective-permute-start.7 = (bf16[128,512]{1,0:T(8,128)(2,1)}, bf16[128,512]{1,0:T(8,128)(2,1)}, u32[]{:S(2)}, u32[]{:S(2)}) collective-permute-start(bf16[128,512]{1,0:T(8,128)(2,1)} %bitcast.53), channel_id=1, source_target_pairs={{0,8},{4,12},{8,0},{12,4},{16,24},{20,28},{24,16},{28,20},{1,9},{5... | collective-permute-start | bytes 393224 | tf_op jit(solution)/shard_map/ppermute | solution.py:900
  57.6 1.9 multiply_sine_fusion
  60.8 9.8 %collective-permute-done.8 = bf16[128,512]{1,0:T(8,128)(2,1)} collective-permute-done((bf16[128,512]{1,0:T(8,128)(2,1)}, bf16[128,512]{1,0:T(8,128)(2,1)}, u32[]{:S(2)}, u32[]{:S(2)}) %collective-permute-start.8) | collective-permute-done | bytes 131104 | tf_op jit(solution)/shard_map/ppermute | solution.py:900
  70.7 2.0 pad_maximum_fusion.7.refs_0_
  74.4 9.2 %collective-permute-done.6.refs_3_ = bf16[3,144,1024]{2,1,0:T(8,128)(2,1)} collective-permute-done((bf16[3,144,1024]{2,1,0:T(8,128)(2,1)}, bf16[3,144,1024]{2,1,0:T(8,128)(2,1)}, u32[]{:S(2)}, u32[]{:S(2)}) %collective-permute-start.6) | collective-permute-done | bytes 884768 | tf_op jit(solution)/shard_map/ppermute | solution.py:900
  85.6 7.4 %shard_map.255 = (bf16[1024,1024]{1,0:T(8,128)(2,1)S(1)}, bf16[1024,512]{1,0:T(8,128)(2,1)S(1)}, bf16[1024,256]{1,0:T(8,128)(2,1)S(1)}, bf16[1024,256]{1,0:T(8,1...) custom-call(s32[1]{0:T(128)} %bitcast.8.member_ref, ...), custom_call_target="tpu_custom_call" | custom-call | flops 4294967296 | tf_op jit(solution)/shard_map/pallas_call | solution.py:344
  95.7 6.9 %shard_map.256 = (bf16[1024,512]{1,0:T(8,128)(2,1)S(1)}, f32[2,2,1024]{2,1,0:T(2,128)S(1)}) custom-call(s32[4]{0:T(128)S(1)} %xor_add_fusion.block_of, bf16[1024,512]{1,0:T(8,128)(2,1)S(1)} %get-tuple-element.113.q_ref, bf16[1024,256]{1,0:T(8,128)(2,1)S(1)} %get-tuple-element.82.k_ref, bf16[1024,256]{1,0:T(8,128)(2,1)S(1)} %get-tuple-element.83.v_ref, ...), custom_call_target="tpu_custom_call" | custom-call | flops 3221225472 | tf_op jit(solution)/shard_map/pallas_call | solution.py:344
  102.7 3.8 %shard_map.257 = (f32[512,1024]{1,0:T(8,128)S(1)}, bf16[512,1024]{1,0:T(8,128)(2,1)S(1)}, bf16[1024,512]{1,0:T(8,128)(2,1)S(1)}) custom-call(s32[1]{0:T(128)} %bitcast.8.member_ref, bf16[1024,512]{1,0:T(8,128)(2,1)S(1)} %get-tuple-element.85.mixed_ref.refs_2_, bf16[4,128,512]{2,1,0:T(8,128)(2,1)} %pad_maximum_fusion.7.refs_0_, ...), custom_call_target="tpu_custom_call" | custom-call | flops 2147483648 | tf_op jit(solution)/shard_map/pallas_call | solution.py:344
  106.5 2.6 collective-permute-done.11
  110.8 24.1 %collective-permute-done.12 = bf16[512,1024]{1,0:T(8,128)(2,1)S(1)} collective-permute-done((bf16[512,1024]{1,0:T(8,128)(2,1)S(1)}, bf16[512,1024]{1,0:T(8,128)(2,1)S(1)}, u32[]{:S(2)}, u32[]{:S(2)}) %collective-permute-start.12) | collective-permute-done | bytes 1048608 | tf_op jit(solution)/shard_map/ppermute | solution.py:900
  135.6 1.8 multiply_convert_fusion
  138.6 1.7 collective-permute-done.13.xb_ref
  143.7 15.9 %shard_map.258 = (bf16[1024,768]{1,0:T(8,128)(2,1)S(1)}, bf16[1024,1536]{1,0:T(8,128)(2,1)}, f32[512,1024]{1,0:T(8,128)S(1)}, bf16[512,1024]{1,0:T(8,128)(2,1)S(1)}) custom-call(s32[1]{0:T(128)} %bitcast.8.member_ref, bf16[512,1024]{1,0:T(8,128)(2,1)S(1)} %copy-done.19, bf16[512,1024]{1,0:T(8,128)(2,1)S(1)} %copy-done.26, bf16[1024,1024]{1,0:T(8,128)(2,1)S(1)} %copy-done.3, ...), custom_call_target="tpu_custom_call" | custom-call | flops 16106127360 | tf_op jit(solution)/shard_map/pallas_call | solution.py:344
  159.8 2.5 collective-permute-done.14
  164.6 9.3 %shard_map.259 = bf16[1024,2304]{1,0:T(8,128)(2,1)} custom-call(s32[1]{0:T(128)} %bitcast.8.member_ref, bf16[512,1024]{1,0:T(8,128)(2,1)S(1)} %copy-done.20, bf16[512,1024]{1,0:T(8,128)(2,1)S(1)} %copy-done.27, bf16[1024,1024]{1,0:T(8,128)(2,1)S(1)} %copy-done.3, bf16[1024,1024]{1,0:T(8,128)(2,1)} %collective-permute-done.5.xb_ref.gb_ref, ...), custom_call_target="tpu_custom_call" | custom-call | flops 9663676416 | tf_op jit(solution)/shard_map/pallas_call | solution.py:344
  173.9 5.7 %fusion = f32[1024,1024]{1,0:T(8,128)} fusion(bf16[1024,768]{1,0:T(8,128)(2,1)} %copy-done.31, bf16[1024,2304]{1,0:T(8,128)(2,1)} %all-gather.2.cloned.1.call-done.gate_up.down_ref), kind=kOutput, calls=%fused_computation.17 | convolution fusion | flops 1610612736 | bytes 7340032 | tf_op jit(solution)/shard_map/dot_general | solution.py:330
  179.7 2.7 slice.323
  183.7 1.7 collective-permute-done.15
  185.4 3.8 %slice_add_fusion = f32[512,1024]{1,0:T(8,128)} fusion(f32[1024,1024]{1,0:T(8,128)} %fusion, bf16[512,1024]{1,0:T(8,128)(2,1)} %collective-permute-done.15), kind=kLoop, calls=%fused_computation.6 | loop fusion | flops 1048576 | bytes 5242880 | tf_op jit(solution)/shard_map/add | solution.py:1070
  189.2 19.1 %collective-permute-done.16 = bf16[512,1024]{1,0:T(8,128)(2,1)} collective-permute-done((bf16[512,1024]{1,0:T(8,128)(2,1)}, bf16[512,1024]{1,0:T(8,128)(2,1)}, u32[]{:S(2)}, u32[]{:S(2)}) %collective-permute-start.16) | collective-permute-done | bytes 1048608 | tf_op jit(solution)/shard_map/ppermute | solution.py:900
  210.3 1.9 fusion.29
  212.2 2.7 collective-permute-done.18.refs_1_.branch_b_ref
  214.9 2.4 shard_map.260
  218.8 9.9 %shard_map.261 = (bf16[1024,256]{1,0:T(8,128)(2,1)S(1)}, bf16[1024,128]{1,0:T(8,128)(2,1)S(1)}, bf16[1024,128]{1,0:T(8,128)(2,1)S(1)}, f32[1,128]{1,0:T(1,128)S(1)}, f32[1,128]{1,0:T(1,128)S(1)}) custom-call(s32[4]{0:T(128)S(1)} %xor_add_fusion.block_of, bf16[1024,512]{1,0:T(8,128)(2,1)S(1)} %copy-done.9, bf16[1024,256]{1,0:T(8,128)(2,1)S(1)} %copy-done.13, ...), custom_call_target="tpu_custom_call" | custom-call | flops 3221225472 | tf_op jit(solution)/shard_map/pallas_call | solution.py:344
  228.7 3.9 %shard_map.262 = (bf16[4,128,512]{2,1,0:T(8,128)(2,1)S(1)}, bf16[4,128,512]{2,1,0:T(8,128)(2,1)}) custom-call(s32[1]{0:T(128)} %bitcast.8.member_ref, bf16[1024,1024]{1,0:T(8,128)(2,1)S(1)} %copy-done.33, bf16[1024,256]{1,0:T(8,128)(2,1)S(1)} %get-tuple-element.119.refs_1_.refs_0_, bf16[1024,128]{1,0:T(8,128)(2,1)S(1)} %get-tuple-element.109.refs_2_, ...), custom_call_target="tpu_custom_call" | custom-call | flops 2147483648 | tf_op jit(solution)/shard_map/pallas_call | solution.py:344
  235.4 9.9 %shard_map.263 = (bf16[1024,256]{1,0:T(8,128)(2,1)S(1)}, bf16[1024,128]{1,0:T(8,128)(2,1)S(1)}, bf16[1024,128]{1,0:T(8,128)(2,1)S(1)}, f32[1,128]{1,0:T(1,128)S(1)}, f32[1,128]{1,0:T(1,128)S(1)}) custom-call(s32[4]{0:T(128)S(1)} %xor_add_fusion.block_of, bf16[1024,512]{1,0:T(8,128)(2,1)S(1)} %copy-done.9, bf16[1024,256]{1,0:T(8,128)(2,1)S(1)} %copy-done.13, ...), custom_call_target="tpu_custom_call" | custom-call | flops 3221225472 | tf_op jit(solution)/shard_map/pallas_call | solution.py:344
  245.3 3.0 shard_map.264
  249.1 7.2 %shard_map.265 = (f32[512,1024]{1,0:T(8,128)S(1)}, bf16[512,1024]{1,0:T(8,128)(2,1)S(1)}, f32[1,1024]{1,0:T(1,128)S(1)}) custom-call(s32[1]{0:T(128)} %bitcast.8.member_ref, bf16[1024,1024]{1,0:T(8,128)(2,1)S(1)} %copy-done.3, bf16[1024,1024]{1,0:T(8,128)(2,1)} %collective-permute-done.5.xb_ref.gb_ref, ...), custom_call_target="tpu_custom_call" | custom-call | flops 4294967296 | tf_op jit(solution)/shard_map/pallas_call | solution.py:344
  257.9 2.5 slice.325
  263.7 11.1 %collective-permute-done.24 = f32[2304]{0:T(1024)S(1)} collective-permute-done((f32[2304]{0:T(1024)S(1)}, f32[2304]{0:T(1024)S(1)}, u32[]{:S(2)}, u32[]{:S(2)}) %collective-permute-start.24) | collective-permute-done | bytes 9248 | tf_op jit(solution)/shard_map/ppermute | solution.py:900
  277.3 5.5 %collective-permute-done.25 = f32[2304]{0:T(1024)S(1)} collective-permute-done((f32[2304]{0:T(1024)S(1)}, f32[2304]{0:T(1024)S(1)}, u32[]{:S(2)}, u32[]{:S(2)}) %collective-permute-start.25) | collective-permute-done | bytes 9248 | tf_op jit(solution)/shard_map/ppermute | solution.py:900
  284.9 2.6 collective-permute-done.26
  287.5 1.6 collective-permute-start.27
  289.2 2.6 fusion.18
  291.8 8.6 %collective-permute-done.27 = f32[2304]{0:T(1024)S(1)} collective-permute-done((f32[2304]{0:T(1024)S(1)}, f32[2304]{0:T(1024)S(1)}, u32[]{:S(2)}, u32[]{:S(2)}) %collective-permute-start.27) | collective-permute-done | bytes 9248 | tf_op jit(solution)/shard_map/ppermute | solution.py:900
  300.6 4.5 %collective-permute-start.30 = (bf16[2,128,512]{2,1,0:T(8,128)(2,1)S(1)}, bf16[2,128,512]{2,1,0:T(8,128)(2,1)S(1)}, u32[]{:S(2)}, u32[]{:S(2)}) collective-permute-start(bf16[2,128,512]{2,1,0:T(8,128)(2,1)S(1)} %slice.326), channel_id=1, source_target_pairs={{0,8},{4,12},{8,0},{12,4},{16,24},{20,28},{24,16},{28,20},{1,9},{5... | collective-permute-start | bytes 786440 | tf_op jit(solution)/shard_map/ppermute | solution.py:900
  305.2 5.3 %collective-permute-done.30 = bf16[2,128,512]{2,1,0:T(8,128)(2,1)S(1)} collective-permute-done((bf16[2,128,512]{2,1,0:T(8,128)(2,1)S(1)}, bf16[2,128,512]{2,1,0:T(8,128)(2,1)S(1)}, u32[]{:S(2)}, u32[]{:S(2)}) %collective-permute-start.30) | collective-permute-done | bytes 262176 | tf_op jit(solution)/shard_map/ppermute | solution.py:900
  312.0 1.7 collective-permute-start.22
  314.2 15.1 %collective-permute-done.31 = bf16[1,128,1536]{2,1,0:T(8,128)(2,1)S(1)} collective-permute-done((bf16[1,128,1536]{2,1,0:T(8,128)(2,1)S(1)}, bf16[1,128,1536]{2,1,0:T(8,128)(2,1)S(1)}, u32[]{:S(2)}, u32[]{:S(2)}) %collective-permute-start.31) | collective-permute-done | bytes 393248 | tf_op jit(solution)/shard_map/ppermute | solution.py:900
  333.4 8.0 %collective-permute-done.32 = f32[64,1536]{1,0:T(8,128)S(1)} collective-permute-done((f32[64,1536]{1,0:T(8,128)S(1)}, f32[64,1536]{1,0:T(8,128)S(1)}, u32[]{:S(2)}, u32[]{:S(2)}) %collective-permute-start.32) | collective-permute-done | bytes 393248 | tf_op jit(solution)/shard_map/ppermute | solution.py:900
  347.8 3.1 collective-permute-done.33
  (250 shorter events, 66.4 us)
Async XLA Ops:
  7.2 15.2 %copy-start = (f32[1536,128]{1,0:T(8,128)S(1)}, f32[1536,128]{1,0:T(8,128)}, u32[]{:S(2)}) copy-start(f32[1536,128]{1,0:T(8,128)} %param.28) | copy-start | bytes 2359300
  7.2 134.1 %all-gather.2.cloned.1.call-start = ((), (), s32[]{:S(2)}) async-start(), calls=%async_computation.1 | async-start | bytes 5308416 | tf_op jit(solution)/shard_map/all_gather | solution.py:983
  10.3 31.4 %collective-permute-start.4 = (bf16[528,1024]{1,0:T(8,128)(2,1)S(1)}, bf16[528,1024]{1,0:T(8,128)(2,1)}, u32[]{:S(2)}, u32[]{:S(2)}) collective-permute-start(bf16[528,1024]{1,0:T(8,128)(2,1)S(1)} %pad_maximum_fusion.2), channel_id=1, source_target_pairs={{0,2},{2,0},{1,3},{3,1},{4,6},{6,4},{5,7},{7,5},{8,10},{10,8},{9,1... | collective-permute-start | bytes 3244040 | tf_op jit(solution)/shard_map/ppermute | solution.py:900
  16.2 14.0 %collective-permute-start = (bf16[144,1024]{1,0:T(8,128)(2,1)S(1)}, bf16[144,1024]{1,0:T(8,128)(2,1)S(1)}, u32[]{:S(2)}, u32[]{:S(2)}) collective-permute-start(bf16[144,1024]{1,0:T(8,128)(2,1)S(1)} %get-tuple-element.166), channel_id=1, source_target_pairs={{0,8},{4,12},{8,0},{12,4},{16,24},{20,28},{24,16},{28,20},{1,9},{5... | collective-permute-start | bytes 884744 | tf_op jit(solution)/shard_map/ppermute | solution.py:900
  18.1 23.6 %collective-permute-start.1 = (bf16[144,1024]{1,0:T(8,128)(2,1)S(1)}, bf16[144,1024]{1,0:T(8,128)(2,1)}, u32[]{:S(2)}, u32[]{:S(2)}) collective-permute-start(bf16[144,1024]{1,0:T(8,128)(2,1)S(1)} %get-tuple-element.166), channel_id=1, source_target_pairs={{0,16},{4,20},{8,24},{12,28},{16,0},{20,4},{24,8},{28,12},{1,17},{... | collective-permute-start | bytes 884744 | tf_op jit(solution)/shard_map/ppermute | solution.py:900
  20.7 21.0 %collective-permute-start.2 = (bf16[144,1024]{1,0:T(8,128)(2,1)S(1)}, bf16[144,1024]{1,0:T(8,128)(2,1)}, u32[]{:S(2)}, u32[]{:S(2)}) collective-permute-start(bf16[144,1024]{1,0:T(8,128)(2,1)S(1)} %get-tuple-element.166), channel_id=1, source_target_pairs={{0,24},{4,28},{8,16},{12,20},{16,8},{20,12},{24,0},{28,4},{1,25},{... | collective-permute-start | bytes 884744 | tf_op jit(solution)/shard_map/ppermute | solution.py:900
  20.7 21.0 %collective-permute-start.3 = (bf16[144,1024]{1,0:T(8,128)(2,1)S(1)}, bf16[144,1024]{1,0:T(8,128)(2,1)S(1)}, u32[]{:S(2)}, u32[]{:S(2)}) collective-permute-start(bf16[144,1024]{1,0:T(8,128)(2,1)S(1)} %get-tuple-element.166), channel_id=1, source_target_pairs={{0,4},{4,0},{8,12},{12,8},{16,20},{20,16},{24,28},{28,24},{1,5},{5... | collective-permute-start | bytes 884744 | tf_op jit(solution)/shard_map/ppermute | solution.py:900
  44.0 298.8 %reduce-scatter.2.cloned.1.call-start = ((), (), s32[]{:S(2)}) async-start(), calls=%async_computation.2 | async-start | bytes 5308416 | tf_op jit(solution)/shard_map/reduce_scatter | solution.py:1068
  45.4 12.2 %copy-start.49 = (s32[1,512]{1,0:T(1,128)S(1)}, s32[1,512]{1,0:T(1,128)}, u32[]{:S(2)}) copy-start(s32[1,512]{1,0:T(1,128)} %param.17) | copy-start | bytes 6148
  45.6 27.0 %copy-start.2 = (bf16[1024,1024]{1,0:T(8,128)(2,1)}, bf16[1024,1024]{1,0:T(8,128)(2,1)S(1)}, u32[]{:S(2)}) copy-start(bf16[1024,1024]{1,0:T(8,128)(2,1)S(1)} %pad_maximum_fusion.1.xa_ref.ga_ref) | copy-start | bytes 6291460
  45.6 28.5 %collective-permute-start.5 = (bf16[1024,1024]{1,0:T(8,128)(2,1)S(1)}, bf16[1024,1024]{1,0:T(8,128)(2,1)}, u32[]{:S(2)}, u32[]{:S(2)}) collective-permute-start(bf16[1024,1024]{1,0:T(8,128)(2,1)S(1)} %pad_maximum_fusion.1.xa_ref.ga_ref), channel_id=1, source_target_pairs={{0,1},{1,0},{2,3},{3,2},{4,5},{5,4},{6,7},{7,6},{8,9},{9,8},{10,11... | collective-permute-start | bytes 6291464 | tf_op jit(solution)/shard_map/ppermute | solution.py:900
  47.7 13.1 %collective-permute-start.7 = (bf16[128,512]{1,0:T(8,128)(2,1)}, bf16[128,512]{1,0:T(8,128)(2,1)}, u32[]{:S(2)}, u32[]{:S(2)}) collective-permute-start(bf16[128,512]{1,0:T(8,128)(2,1)} %bitcast.53), channel_id=1, source_target_pairs={{0,8},{4,12},{8,0},{12,4},{16,24},{20,28},{24,16},{28,20},{1,9},{5... | collective-permute-start | bytes 393224 | tf_op jit(solution)/shard_map/ppermute | solution.py:900
  52.9 17.8 %collective-permute-start.8 = (bf16[128,512]{1,0:T(8,128)(2,1)}, bf16[128,512]{1,0:T(8,128)(2,1)}, u32[]{:S(2)}, u32[]{:S(2)}) collective-permute-start(bf16[128,512]{1,0:T(8,128)(2,1)} %bitcast.53), channel_id=1, source_target_pairs={{0,16},{4,20},{8,24},{12,28},{16,0},{20,4},{24,8},{28,12},{1,17},{... | collective-permute-start | bytes 393224 | tf_op jit(solution)/shard_map/ppermute | solution.py:900
  54.0 16.7 %collective-permute-start.9 = (bf16[128,512]{1,0:T(8,128)(2,1)}, bf16[128,512]{1,0:T(8,128)(2,1)}, u32[]{:S(2)}, u32[]{:S(2)}) collective-permute-start(bf16[128,512]{1,0:T(8,128)(2,1)} %bitcast.53), channel_id=1, source_target_pairs={{0,24},{4,28},{8,16},{12,20},{16,8},{20,12},{24,0},{28,4},{1,25},{... | collective-permute-start | bytes 393224 | tf_op jit(solution)/shard_map/ppermute | solution.py:900
  55.4 28.2 %collective-permute-start.6 = (bf16[3,144,1024]{2,1,0:T(8,128)(2,1)}, bf16[3,144,1024]{2,1,0:T(8,128)(2,1)}, u32[]{:S(2)}, u32[]{:S(2)}) collective-permute-start(bf16[3,144,1024]{2,1,0:T(8,128)(2,1)} %pad_maximum_fusion.3.refs_1_), channel_id=1, source_target_pairs={{0,4},{4,0},{8,12},{12,8},{16,20},{20,16},{24,28},{28,24},{1,5},{5... | collective-permute-start | bytes 2654216 | tf_op jit(solution)/shard_map/ppermute | solution.py:900
  72.6 30.0 %collective-permute-start.10 = (bf16[4,128,512]{2,1,0:T(8,128)(2,1)}, bf16[4,128,512]{2,1,0:T(8,128)(2,1)}, u32[]{:S(2)}, u32[]{:S(2)}) collective-permute-start(bf16[4,128,512]{2,1,0:T(8,128)(2,1)} %pad_maximum_fusion.7.refs_0_), channel_id=1, source_target_pairs={{0,4},{4,0},{8,12},{12,8},{16,20},{20,16},{24,28},{28,24},{1,5},{5... | collective-permute-start | bytes 1572872 | tf_op jit(solution)/shard_map/ppermute | solution.py:900
  106.5 2.7 collective-permute-start.11
  109.6 25.4 %copy-start.3 = (bf16[1024,1024]{1,0:T(8,128)(2,1)S(1)}, bf16[1024,1024]{1,0:T(8,128)(2,1)}, u32[]{:S(2)}) copy-start(bf16[1024,1024]{1,0:T(8,128)(2,1)} %copy-done.2) | copy-start | bytes 6291460
  109.6 25.3 %collective-permute-start.12 = (bf16[512,1024]{1,0:T(8,128)(2,1)S(1)}, bf16[512,1024]{1,0:T(8,128)(2,1)S(1)}, u32[]{:S(2)}, u32[]{:S(2)}) collective-permute-start(bf16[512,1024]{1,0:T(8,128)(2,1)S(1)} %fusion.2), channel_id=1, source_target_pairs={{0,2},{2,0},{1,3},{3,1},{4,6},{6,4},{5,7},{7,5},{8,10},{10,8},{9,1... | collective-permute-start | bytes 3145736 | tf_op jit(solution)/shard_map/ppermute | solution.py:900
  137.7 2.7 collective-permute-start.13
  159.7 2.7 collective-permute-start.14
  182.4 3.0 collective-permute-start.15
  182.5 25.8 %collective-permute-start.16 = (bf16[512,1024]{1,0:T(8,128)(2,1)}, bf16[512,1024]{1,0:T(8,128)(2,1)}, u32[]{:S(2)}, u32[]{:S(2)}) collective-permute-start(bf16[512,1024]{1,0:T(8,128)(2,1)} %fusion.3), channel_id=1, source_target_pairs={{0,2},{2,0},{1,3},{3,1},{4,6},{6,4},{5,7},{7,5},{8,10},{10,8},{9,1... | collective-permute-start | bytes 3145736 | tf_op jit(solution)/shard_map/ppermute | solution.py:900
  185.4 24.2 %copy-start.37 = (f32[512,1024]{1,0:T(8,128)S(1)}, f32[512,1024]{1,0:T(8,128)}, u32[]{:S(2)}) copy-start(f32[512,1024]{1,0:T(8,128)} %get-tuple-element.134) | copy-start | bytes 6291460
  185.4 24.2 %copy-start.46 = (bf16[512,1024]{1,0:T(8,128)(2,1)S(1)}, bf16[512,1024]{1,0:T(8,128)(2,1)}, u32[]{:S(2)}) copy-start(bf16[512,1024]{1,0:T(8,128)(2,1)} %copy-done.45) | copy-start | bytes 3145732
  189.2 20.5 %copy-start.5 = (f32[512,1024]{1,0:T(8,128)S(1)}, f32[512,1024]{1,0:T(8,128)}, u32[]{:S(2)}) copy-start(f32[512,1024]{1,0:T(8,128)} %copy-done.4) | copy-start | bytes 6291460
  212.2 2.7 collective-permute-start.18
  217.4 17.0 %collective-permute-start.19 = (bf16[4,128,512]{2,1,0:T(8,128)(2,1)S(1)}, bf16[4,128,512]{2,1,0:T(8,128)(2,1)S(1)}, u32[]{:S(2)}, u32[]{:S(2)}) collective-permute-start(bf16[4,128,512]{2,1,0:T(8,128)(2,1)S(1)} %get-tuple-element.102), channel_id=1, source_target_pairs={{0,4},{4,0},{8,12},{12,8},{16,20},{20,16},{24,28},{28,24},{1,5},{5... | collective-permute-start | bytes 1572872 | tf_op jit(solution)/shard_map/ppermute | solution.py:900
  233.4 42.6 %collective-permute-start.20 = (bf16[4,128,512]{2,1,0:T(8,128)(2,1)}, bf16[4,128,512]{2,1,0:T(8,128)(2,1)}, u32[]{:S(2)}, u32[]{:S(2)}) collective-permute-start(bf16[4,128,512]{2,1,0:T(8,128)(2,1)} %get-tuple-element.112), channel_id=1, source_target_pairs={{0,4},{4,0},{8,12},{12,8},{16,20},{20,16},{24,28},{28,24},{1,5},{5... | collective-permute-start | bytes 1572872 | tf_op jit(solution)/shard_map/ppermute | solution.py:900
  249.1 26.9 %copy-start.22 = (bf16[4,128,512]{2,1,0:T(8,128)(2,1)S(1)}, bf16[4,128,512]{2,1,0:T(8,128)(2,1)}, u32[]{:S(2)}) copy-start(bf16[4,128,512]{2,1,0:T(8,128)(2,1)} %copy-done.21) | copy-start | bytes 1572868
  257.7 26.4 %copy-start.43 = (f32[4,128,512]{2,1,0:T(8,128)S(1)}, f32[4,128,512]{2,1,0:T(8,128)}, u32[]{:S(2)}) copy-start(f32[4,128,512]{2,1,0:T(8,128)} %convert_add_fusion.7) | copy-start | bytes 3145732
  257.7 3.9 %collective-permute-start.23 = (f32[2304]{0:T(1024)S(1)}, f32[2304]{0:T(1024)S(1)}, u32[]{:S(2)}, u32[]{:S(2)}) collective-permute-start(f32[2304]{0:T(1024)S(1)} %pad_maximum_fusion.9), channel_id=1, source_target_pairs={{0,1},{1,0},{2,3},{3,2},{4,5},{5,4},{6,7},{7,6},{8,9},{9,8},{10,11... | collective-permute-start | bytes 27656 | tf_op jit(solution)/shard_map/ppermute | solution.py:900
  260.5 28.7 %collective-permute-start.17 = (bf16[256,1024]{1,0:T(8,128)(2,1)}, bf16[256,1024]{1,0:T(8,128)(2,1)}, u32[]{:S(2)}, u32[]{:S(2)}) collective-permute-start(bf16[256,1024]{1,0:T(8,128)(2,1)} %slice.325), channel_id=1, source_target_pairs={{0,2},{2,0},{1,3},{3,1},{4,6},{6,4},{5,7},{7,5},{8,10},{10,8},{9,1... | collective-permute-start | bytes 1572872 | tf_op jit(solution)/shard_map/ppermute | solution.py:900
  261.6 13.3 %collective-permute-start.24 = (f32[2304]{0:T(1024)S(1)}, f32[2304]{0:T(1024)S(1)}, u32[]{:S(2)}, u32[]{:S(2)}) collective-permute-start(f32[2304]{0:T(1024)S(1)} %fusion.27), channel_id=1, source_target_pairs={{0,2},{2,0},{1,3},{3,1},{4,6},{6,4},{5,7},{7,5},{8,10},{10,8},{9,1... | collective-permute-start | bytes 27656 | tf_op jit(solution)/shard_map/ppermute | solution.py:900
  262.6 37.8 %collective-permute-start.29 = (bf16[4,128,512]{2,1,0:T(8,128)(2,1)}, bf16[4,128,512]{2,1,0:T(8,128)(2,1)S(1)}, u32[]{:S(2)}, u32[]{:S(2)}) collective-permute-start(bf16[4,128,512]{2,1,0:T(8,128)(2,1)} %copy-done.28), channel_id=1, source_target_pairs={{0,4},{4,0},{8,12},{12,8},{16,20},{20,16},{24,28},{28,24},{1,5},{5... | collective-permute-start | bytes 1572872 | tf_op jit(solution)/shard_map/ppermute | solution.py:900
  274.9 14.3 %copy-start.39 = (f32[512,1024]{1,0:T(8,128)S(1)}, f32[512,1024]{1,0:T(8,128)}, u32[]{:S(2)}) copy-start(f32[512,1024]{1,0:T(8,128)} %copy-done.38) | copy-start | bytes 6291460
  274.9 7.9 %collective-permute-start.25 = (f32[2304]{0:T(1024)S(1)}, f32[2304]{0:T(1024)S(1)}, u32[]{:S(2)}, u32[]{:S(2)}) collective-permute-start(f32[2304]{0:T(1024)S(1)} %add.183), channel_id=1, source_target_pairs={{0,4},{4,0},{8,12},{12,8},{16,20},{20,16},{24,28},{28,24},{1,5},{5... | collective-permute-start | bytes 27656 | tf_op jit(solution)/shard_map/ppermute | solution.py:900
  282.7 4.8 %collective-permute-start.26 = (f32[2304]{0:T(1024)S(1)}, f32[2304]{0:T(1024)S(1)}, u32[]{:S(2)}, u32[]{:S(2)}) collective-permute-start(f32[2304]{0:T(1024)S(1)} %add.184), channel_id=1, source_target_pairs={{0,8},{4,12},{8,0},{12,4},{16,24},{20,28},{24,16},{28,20},{1,9},{5... | collective-permute-start | bytes 27656 | tf_op jit(solution)/shard_map/ppermute | solution.py:900
  284.2 20.9 %collective-permute-start.28 = (bf16[2,128,1024]{2,1,0:T(8,128)(2,1)S(1)}, bf16[2,128,1024]{2,1,0:T(8,128)(2,1)S(1)}, u32[]{:S(2)}, u32[]{:S(2)}) collective-permute-start(bf16[2,128,1024]{2,1,0:T(8,128)(2,1)S(1)} %fusion.14), channel_id=1, source_target_pairs={{0,8},{4,12},{8,0},{12,4},{16,24},{20,28},{24,16},{28,20},{1,9},{5... | collective-permute-start | bytes 1572872 | tf_op jit(solution)/shard_map/ppermute | solution.py:900
  284.9 26.5 %collective-permute-start.21 = (bf16[512,1024]{1,0:T(8,128)(2,1)S(1)}, bf16[512,1024]{1,0:T(8,128)(2,1)S(1)}, u32[]{:S(2)}, u32[]{:S(2)}) collective-permute-start(bf16[512,1024]{1,0:T(8,128)(2,1)S(1)} %copy-done.24), channel_id=1, source_target_pairs={{0,1},{1,0},{2,3},{3,2},{4,5},{5,4},{6,7},{7,6},{8,9},{9,8},{10,11... | collective-permute-start | bytes 3145736 | tf_op jit(solution)/shard_map/ppermute | solution.py:900
  287.5 12.9 %collective-permute-start.27 = (f32[2304]{0:T(1024)S(1)}, f32[2304]{0:T(1024)S(1)}, u32[]{:S(2)}, u32[]{:S(2)}) collective-permute-start(f32[2304]{0:T(1024)S(1)} %add.185), channel_id=1, source_target_pairs={{0,16},{4,20},{8,24},{12,28},{16,0},{20,4},{24,8},{28,12},{1,17},{... | collective-permute-start | bytes 27656 | tf_op jit(solution)/shard_map/ppermute | solution.py:900
  300.6 9.9 %collective-permute-start.30 = (bf16[2,128,512]{2,1,0:T(8,128)(2,1)S(1)}, bf16[2,128,512]{2,1,0:T(8,128)(2,1)S(1)}, u32[]{:S(2)}, u32[]{:S(2)}) collective-permute-start(bf16[2,128,512]{2,1,0:T(8,128)(2,1)S(1)} %slice.326), channel_id=1, source_target_pairs={{0,8},{4,12},{8,0},{12,4},{16,24},{20,28},{24,16},{28,20},{1,9},{5... | collective-permute-start | bytes 786440 | tf_op jit(solution)/shard_map/ppermute | solution.py:900
  310.6 18.7 %collective-permute-start.31 = (bf16[1,128,1536]{2,1,0:T(8,128)(2,1)S(1)}, bf16[1,128,1536]{2,1,0:T(8,128)(2,1)S(1)}, u32[]{:S(2)}, u32[]{:S(2)}) collective-permute-start(bf16[1,128,1536]{2,1,0:T(8,128)(2,1)S(1)} %fusion.22), channel_id=1, source_target_pairs={{0,16},{4,20},{8,24},{12,28},{16,0},{20,4},{24,8},{28,12},{1,17},{... | collective-permute-start | bytes 1179656 | tf_op jit(solution)/shard_map/ppermute | solution.py:900
  311.9 17.6 %copy-start.42 = (bf16[1,256,1024]{2,1,0:T(8,128)(2,1)S(1)}, bf16[1,256,1024]{2,1,0:T(8,128)(2,1)}, u32[]{:S(2)}) copy-start(bf16[1,256,1024]{2,1,0:T(8,128)(2,1)} %param.16) | copy-start | bytes 1572868
  312.0 17.5 %collective-permute-start.22 = (bf16[256,1024]{1,0:T(8,128)(2,1)S(1)}, bf16[256,1024]{1,0:T(8,128)(2,1)S(1)}, u32[]{:S(2)}, u32[]{:S(2)}) collective-permute-start(bf16[256,1024]{1,0:T(8,128)(2,1)S(1)} %slice.324), channel_id=1, source_target_pairs={{0,2},{2,0},{1,3},{3,1},{4,6},{6,4},{5,7},{7,5},{8,10},{10,8},{9,1... | collective-permute-start | bytes 1572872 | tf_op jit(solution)/shard_map/ppermute | solution.py:900
  314.2 15.6 %copy-start.44 = (f32[512,1024]{1,0:T(8,128)S(1)}, f32[512,1024]{1,0:T(8,128)}, u32[]{:S(2)}) copy-start(f32[512,1024]{1,0:T(8,128)} %get-tuple-element.130) | copy-start | bytes 6291460
  331.2 10.1 %collective-permute-start.32 = (f32[64,1536]{1,0:T(8,128)S(1)}, f32[64,1536]{1,0:T(8,128)S(1)}, u32[]{:S(2)}, u32[]{:S(2)}) collective-permute-start(f32[64,1536]{1,0:T(8,128)S(1)} %constant_dynamic-slice_fusion.1), channel_id=1, source_target_pairs={{0,2},{2,0},{1,3},{3,1},{4,6},{6,4},{5,7},{7,5},{8,10},{10,8},{9,1... | collective-permute-start | bytes 1179656 | tf_op jit(solution)/shard_map/ppermute | solution.py:900
  343.8 7.1 %collective-permute-start.33 = (bf16[64,2304]{1,0:T(8,128)(2,1)S(1)}, bf16[64,2304]{1,0:T(8,128)(2,1)S(1)}, u32[]{:S(2)}, u32[]{:S(2)}) collective-permute-start(bf16[64,2304]{1,0:T(8,128)(2,1)S(1)} %constant_dynamic-slice_fusion), channel_id=1, source_target_pairs={{0,2},{2,0},{1,3},{3,1},{4,6},{6,4},{5,7},{7,5},{8,10},{10,8},{9,1... | collective-permute-start | bytes 884744 | tf_op jit(solution)/shard_map/ppermute | solution.py:900
  (44 other events, 168.6 us)
Sparse Core Ops, SparseCore 0:
  44.1 91.5 all-gather.1
  183.8 111.1 reduce-scatter.1
